TPU v7x, 32 devices: a whole 2x2x4 slice. The times are simulated.
32 devices in a mesh: wide: 16 (over z, y, x), narrow: 2 (over core).
Axes of the slice: x: 2, y: 2, z: 4, core: 2. Of those that a mesh axis runs over, the one named last changes fastest.
Arguments:
- tokens: bfloat16 [16, 12288, 512], P('narrow', 'wide')
- cotangent: bfloat16 [16, 12288, 512], P('narrow', 'wide'), may hold values from -6 to 6
- owner_list: int32 [12], replicated, may hold values from 0 to 15, as said below
- master: float32 [16, 512, 512], P('wide', 'narrow')
- moment_one: float32 [16, 512, 512], P('wide', 'narrow'), may hold values from -112 to 112
- moment_two: float32 [16, 512, 512], P('wide', 'narrow'), may hold values from 825.7536 to 13172.736
- small_params: float32 [4608], replicated
- small_one: float32 [4608], replicated, may hold values from -128 to 128
- small_two: float32 [4608], replicated, may hold values from 1297.6128 to 20643.84
Outputs:
- block_out: bfloat16 [16, 12288, 512], P('narrow', 'wide')
- grad_tokens: float32 [16, 12288, 512], P('narrow', 'wide')
- new_master: float32 [16, 512, 512], P('wide', 'narrow')
- new_one: float32 [16, 512, 512], P('wide', 'narrow')
- new_two: float32 [16, 512, 512], P('wide', 'narrow')
- small_new: float32 [4608], replicated
- small_one_new: float32 [4608], replicated
- small_two_new: float32 [4608], replicated
Inputs may be any that keep to these rules, and one draw needn't show every extreme that they name: `owner_list`: 12 different slot indices; 0 and 15 are always among them.
All inputs are finite; a program needn't handle non-finite values.
Results may differ from a plain program's by a relative error of at most 0.025.
Values may be sent and summed in bfloat16 or wider, within the bound.
No kernel may reach another device: no remote copies, remote signals or barrier semaphores. Data moves between devices by JAX's collectives and lax.ppermute only.
A program may use at most 512 MiB of HBM per device.

v0:
```python
import functools
import functools
import itertools
import math

import jax
import jax.numpy as jnp
from jax import lax
from jax.experimental import pallas as pl
from jax.experimental.pallas import tpu as pltpu
from jax.sharding import PartitionSpec as P

D = 512
HEADS = 8
HD = 64
PAIR = 2 * HD
PAIRS = HEADS // 2
FF = 2048
NF = FF // D
ROW = 192
ROWS_IMG = 64
KEYS = ROW + ROWS_IMG
STEP = 10
RATE = 0.03
GAIN_RATE = 0.4
EPS = 1e-05
LOG2E = math.log2(math.e)
F32 = jnp.float32
BF16 = jnp.bfloat16
MIB = 1024 * 1024


def dot(left, right):
    return jnp.dot(left, right, preferred_element_type=F32)


def dot_nt(left, right):
    return lax.dot_general(left, right, (((1,), (1,)), ((), ())), preferred_element_type=F32)


def normalize(values):
    centred = values - jnp.mean(values, -1, keepdims=True)
    scale = lax.rsqrt(jnp.mean(centred * centred, -1, keepdims=True) + EPS)
    return centred * scale, scale


def head_masks(dtype):
    lane = lax.broadcasted_iota(jnp.int32, (1, PAIR), 1)
    first = (lane < HD).astype(F32)
    return first.astype(dtype), (1.0 - first).astype(dtype)


def tile_spec(*tail, buffers=None):
    zeros = (0,) * len(tail)
    return pl.BlockSpec((1,) + tail, lambda step, *_: (step,) + zeros)


def two_spec(*tail):
    zeros = (0,) * len(tail)
    return pl.BlockSpec((2,) + tail, lambda step, *_: (step,) + zeros)


def whole_spec(shape):
    zeros = (0,) * len(shape)
    return pl.BlockSpec(shape, lambda step, *_: zeros, pipeline_mode=pl.Buffered(1))


def weight_spec(block):
    return pl.BlockSpec(
        (1, D, D), lambda step, owner, *_: (owner[block], 0, 0), pipeline_mode=pl.Buffered(1)
    )


def out_whole(shape):
    zeros = (0,) * len(shape)
    return pl.BlockSpec(shape, lambda step, *_: zeros)


def with_ones(rows):
    return jnp.concatenate([rows, jnp.ones((16, rows.shape[1]), rows.dtype)], 0)


def norm_kernel(x_ref, xh_ref, scale_ref, mean_ref):
    normal, scale_ref[0] = normalize(x_ref[0].astype(F32))
    xh_ref[0] = normal.astype(BF16)
    for row in range(mean_ref.shape[1]):
        part = normal[row * ROW : (row + 1) * ROW]
        mean_ref[0, row : row + 1, :] = jnp.mean(part, 0, keepdims=True).astype(BF16)


def norm_call(tokens):
    images, count, _ = tokens.shape
    rows = count // ROW
    return pl.pallas_call(
        norm_kernel,
        grid=(images,),
        in_specs=[tile_spec(count, D)],
        out_specs=[tile_spec(count, D), tile_spec(count, 1), tile_spec(rows, D)],
        out_shape=[
            jax.ShapeDtypeStruct((images, count, D), BF16),
            jax.ShapeDtypeStruct((images, count, 1), F32),
            jax.ShapeDtypeStruct((images, rows, D), BF16),
        ],
        compiler_params=pltpu.CompilerParams(vmem_limit_bytes=60 * MIB),
        cost_estimate=pl.CostEstimate(
            flops=images * count * D * 10, bytes_accessed=images * count * D * 4, transcendentals=0
        ),
        name="norm_one",
    )(tokens)


def group_sizes(wide):
    inner = min(4, wide)
    return inner, wide // inner


def write_pieces(place, out_refs, read):
    narrow = len(out_refs)
    *lead, height, _ = out_refs[0].shape
    wide = math.prod(lead)
    depth = D // narrow // wide

    def one(number, carry):
        for step, out_ref in enumerate(out_refs):
            device = number if len(lead) == 1 else place[0] ^ number
            start = (place[1] ^ step) * (D // narrow) + device * depth
            here = pl.ds(pl.multiple_of(start, depth), depth)
            index = (number,) if len(lead) == 1 else (number % lead[0], number // lead[0])
            for block in range(height // depth):
                value = read(block, here).astype(BF16)
                out_ref[index + (slice(block * depth, (block + 1) * depth), slice(None))] = value
        return carry

    lax.fori_loop(0, wide, one, 0)


def attend_kernel(
    parts, place, xh_ref, mean_ref, params_ref, *refs
):
    g_ref, s_ref = params_ref.at[:, 0:D], params_ref.at[:, D : 2 * D]
    part_refs, refs = refs[:parts], refs[parts:]
    q_ref, k_ref, v_ref, e_ref, o_ref, li_ref, sk_ref, sv_ref, bias_ref, w_ref = refs
    rows = xh_ref.shape[1] // ROW
    first_row = place[0] * rows

    @pl.when(pl.program_id(0) == 0)
    def _():
        query = lax.broadcasted_iota(jnp.int32, (ROW, KEYS), 0)
        key = lax.broadcasted_iota(jnp.int32, (ROW, KEYS), 1)
        summary = jnp.maximum(key - ROW, 0)
        image_row = (place[0] ^ lax.div(summary, rows)) * rows + lax.rem(summary, rows)
        for row in range(rows):
            own = jnp.where(key <= query, 0.0, -1e30)
            earlier = jnp.where(image_row < first_row + row, math.log2(ROW), -1e30)
            bias_ref[row] = jnp.where(key < ROW, own, earlier)
        if parts == 1:
            w_ref[...] = part_refs[0][...]
            return
        wide, height, _ = part_refs[0].shape
        depth = D // parts // wide

        def one(distance, carry):
            for step, part_ref in enumerate(part_refs):
                start = (place[1] ^ step) * (D // parts) + (place[0] ^ distance) * depth
                here = pl.ds(pl.multiple_of(start, depth), depth)
                for block in range(3):
                    w_ref[block, here, :] = part_ref[distance, block * depth : (block + 1) * depth, :]
            return carry

        lax.fori_loop(0, wide, one, 0)

    a1 = (xh_ref[0].astype(F32) * g_ref[...] + s_ref[...]).astype(BF16)
    q_ref[0] = dot(a1, w_ref[0]).astype(BF16)
    k_ref[0] = dot(a1, w_ref[1]).astype(BF16)
    v_ref[0] = dot(a1, w_ref[2]).astype(BF16)
    mean_a = (mean_ref[0].astype(F32) * g_ref[...] + s_ref[...]).astype(BF16)
    sum_k = dot(mean_a, w_ref[1]).astype(BF16)
    sum_v = dot(mean_a, w_ref[2]).astype(BF16)
    sk_ref[0] = sum_k
    sv_ref[0] = sum_v
    masks = head_masks(BF16)
    ones = [jnp.broadcast_to(mask, (KEYS, PAIR)) for mask in masks]
    scale = LOG2E / math.sqrt(HD)

    for row in range(rows):
        here = slice(row * ROW, (row + 1) * ROW)
        for pair in range(PAIRS):
            lanes = slice(pair * PAIR, (pair + 1) * PAIR)
            query = q_ref[0, here, lanes]
            keys = jnp.concatenate([k_ref[0, here, lanes], sum_k[:, lanes]], 0)
            values = jnp.concatenate([v_ref[0, here, lanes], sum_v[:, lanes]], 0)
            total = None
            for half in range(2):
                score = dot_nt(query, keys * masks[half]) * scale + bias_ref[row]
                weight = jnp.exp2(score - jnp.max(score, -1, keepdims=True)).astype(BF16)
                e_ref[0, row, 2 * pair + half] = weight
                part = dot(weight, jnp.concatenate([values * masks[half], ones[half]], 1))
                total = part if total is None else total + part
            inverse = 1.0 / total[:, PAIR:]
            o_ref[0, here, lanes] = (total[:, :PAIR] * inverse).astype(BF16)
            li_ref[0, here, lanes] = inverse.astype(BF16)


def attend_call(place, normal, mean_all, params, parts):
    images, count, _ = normal.shape
    rows = count // ROW
    tokens_shape = jax.ShapeDtypeStruct((images, count, D), BF16)
    return pl.pallas_call(
        functools.partial(attend_kernel, len(parts)),
        grid_spec=pltpu.PrefetchScalarGridSpec(
            num_scalar_prefetch=1,
            grid=(images,),
            in_specs=[
                tile_spec(count, D), tile_spec(ROWS_IMG, D), whole_spec(params.shape),
            ]
            + [whole_spec(part.shape) for part in parts],
            out_specs=[tile_spec(count, D)] * 3
            + [tile_spec(rows, HEADS, ROW, KEYS)]
            + [tile_spec(count, D)] * 2
            + [tile_spec(ROWS_IMG, D)] * 2,
            scratch_shapes=[
                pltpu.VMEM((rows, ROW, KEYS), F32),
                pltpu.VMEM((3, D, D), BF16),
            ],
        ),
        out_shape=[tokens_shape] * 3
        + [jax.ShapeDtypeStruct((images, rows, HEADS, ROW, KEYS), BF16)]
        + [tokens_shape] * 2
        + [jax.ShapeDtypeStruct((images, ROWS_IMG, D), BF16)] * 2,
        compiler_params=pltpu.CompilerParams(vmem_limit_bytes=60 * MIB),
        cost_estimate=pl.CostEstimate(
            flops=images * count * D * D * 10, bytes_accessed=images * count * D * 20, transcendentals=0
        ),
        name="attend",
    )(place, normal, mean_all, params, *parts)


def ff_kernel(
    pieces, owner, place, x_ref, o_ref, cot_ref, li_ref, params_ref,
    wo_ref, u0_ref, u1_ref, u2_ref, u3_ref, d0_ref, d1_ref, d2_ref, d3_ref,
    out_ref, dr_ref, do_ref, small_ref, *refs
):
    grads_refs, (acc_ref, h_ref, xh_ref, act_ref, dp_ref) = refs[:-5], refs[-5:]
    gg_ref, gs_ref = small_ref.at[:, 0:D], small_ref.at[:, D : 2 * D]
    gbu_ref, gbd_ref = small_ref.at[:, 2 * D : 2 * D + FF], small_ref.at[:, 2 * D + FF :]
    g_ref, s_ref = params_ref.at[:, 2 * D : 3 * D], params_ref.at[:, 3 * D : 4 * D]
    bu_ref, bd_ref = params_ref.at[:, 4 * D : 4 * D + FF], params_ref.at[:, 4 * D + FF :]
    step = pl.program_id(0)
    ups = (u0_ref, u1_ref, u2_ref, u3_ref)
    downs = (d0_ref, d1_ref, d2_ref, d3_ref)

    @pl.when(step == 0)
    def _():
        acc_ref[...] = jnp.zeros_like(acc_ref)
        small_ref[...] = jnp.zeros_like(small_ref)

    hidden = x_ref[0].astype(F32) + dot(o_ref[0], wo_ref[0])
    normal, spread = normalize(hidden)
    xh_ref[...] = normal
    h_ref[...] = hidden + bd_ref[...]
    a2 = (normal * g_ref[...] + s_ref[...]).astype(BF16)
    a2_t = a2.T
    cot = cot_ref[0]
    cot_t = cot.T
    c_one = math.sqrt(2.0 / math.pi)
    c_two = c_one * 0.044715
    width = D // 2
    a2_ones = with_ones(a2_t)

    def first_products(start):
        block, inside = start // D, slice(start % D, start % D + width)
        pre = dot(a2, ups[block][0, :, inside]) + bu_ref[:, start : start + width]
        return pre, dot_nt(cot, downs[block][0, inside, :])

    following = first_products(0)
    for start in range(0, FF, width):
        block, inside, columns = start // D, slice(start % D, start % D + width), slice(start, start + width)
        pre, d_act = following
        if start + width < FF:
            following = first_products(start + width)
        square = pre * pre
        half = 0.5 + 0.5 * jnp.tanh(pre * (c_one + c_two * square))
        act = (pre * half).astype(BF16)
        rest = (1.0 - half).astype(BF16)
        half = half.astype(BF16)
        slope = half + act * rest * (2.0 * c_one + (6.0 * c_two) * square.astype(BF16))
        d_pre = d_act.astype(BF16) * slope
        act_ref[:, columns] = act
        dp_ref[:, columns] = d_pre
        part = dot(a2_ones, d_pre)
        acc_ref[1 + block, :, inside] += part[:D]
        gbu_ref[:, columns] += part[D : D + 1]
        acc_ref[1 + NF + block, :, inside] += dot(cot_t, act)
    d_a2 = dot_nt(dp_ref[:, 0:D], ups[0][0])
    for block in range(1, NF):
        d_a2 += dot_nt(dp_ref[:, block * D : (block + 1) * D], ups[block][0])
    normal = xh_ref[...]
    gs_ref[...] += jnp.sum(d_a2, 0, keepdims=True)
    gg_ref[...] += jnp.sum(d_a2 * normal, 0, keepdims=True)
    d_normal = d_a2 * g_ref[...]
    middle = jnp.mean(d_normal, -1, keepdims=True)
    along = jnp.mean(d_normal * normal, -1, keepdims=True)
    cot = cot.astype(F32)
    gbd_ref[...] += jnp.sum(cot, 0, keepdims=True)
    d_hidden = cot + spread * (d_normal - middle - normal * along)
    branch = d_hidden.astype(BF16)
    dr_ref[0] = branch
    total = h_ref[...]
    for block, down in enumerate(downs):
        total += dot(act_ref[:, block * D : (block + 1) * D], down[0])
    out_ref[0] = total.astype(BF16)
    acc_ref[0] += dot(o_ref[0].T, branch)
    do_ref[0] = (dot_nt(branch, wo_ref[0]) * li_ref[0].astype(F32)).astype(BF16)

    @pl.when(step == pl.num_programs(0) - 1)
    def _():
        for block in range(1 + NF, 1 + 2 * NF):
            acc_ref[block] = acc_ref[block].T
        if pieces:
            write_pieces(place, grads_refs, lambda block, here: acc_ref[block, here, :])
        else:
            grads_refs[0][...] = acc_ref[...].astype(BF16)


def grad_shapes(groups, blocks, lead):
    if groups is None:
        return [(blocks, D, D)]
    narrow, wide = groups
    return [lead + (blocks * (D // narrow // wide), D)] * narrow


def ff_call(owner, place, groups, tokens, attended, cotangent, inverse, params, slots):
    images, count, _ = tokens.shape
    tokens_shape = jax.ShapeDtypeStruct((images, count, D), BF16)
    blocks = 1 + 2 * NF
    grads = grad_shapes(groups, blocks, groups and groups[1:])
    return pl.pallas_call(
        functools.partial(ff_kernel, groups is not None),
        grid_spec=pltpu.PrefetchScalarGridSpec(
            num_scalar_prefetch=2,
            grid=(images,),
            in_specs=[tile_spec(count, D)] * 4
            + [whole_spec(params.shape)]
            + [weight_spec(3 + block) for block in range(blocks)],
            out_specs=[tile_spec(count, D)] * 3
            + [out_whole((1, 3 * D + FF))]
            + [out_whole(shape) for shape in grads],
            scratch_shapes=[
                pltpu.VMEM((blocks, D, D), F32),
                pltpu.VMEM((count, D), F32),
                pltpu.VMEM((count, D), F32),
                pltpu.VMEM((count, FF), BF16),
                pltpu.VMEM((count, FF), BF16),
            ],
        ),
        out_shape=[tokens_shape] * 3
        + [jax.ShapeDtypeStruct((1, 3 * D + FF), F32)]
        + [jax.ShapeDtypeStruct(shape, BF16) for shape in grads],
        compiler_params=pltpu.CompilerParams(vmem_limit_bytes=60 * MIB),
        cost_estimate=pl.CostEstimate(
            flops=images * count * D * D * 54, bytes_accessed=images * count * D * 14, transcendentals=0
        ),
        name="feed_forward",
    )(owner, place, tokens, attended, cotangent, inverse, params, *([slots] * blocks))


def back_kernel(pieces, owner, place, *refs):
    (q_ref, k_ref, v_ref, o_ref, do_ref, e_ref, xh_ref, sk_ref, sv_ref, mean_ref, params_ref) = refs[:11]
    weights = refs[11:14]
    grad_ref, dm_ref, small_ref, *grads_refs = refs[14:-3]
    acc_ref, dsk_ref, dsv_ref = refs[-3:]
    step = pl.program_id(0)
    rows = q_ref.shape[1] // ROW
    scale = 1.0 / math.sqrt(HD)

    @pl.when(step == 0)
    def _():
        acc_ref[...] = jnp.zeros_like(acc_ref)

    sum_k = sk_ref[0]
    sum_v = sv_ref[0]
    masks = head_masks(BF16)
    blank = jnp.zeros((HD, KEYS), BF16)
    minus = jnp.full((HD, KEYS), -1.0, BF16)
    d_sum_k = jnp.zeros((ROWS_IMG, D), F32)
    d_sum_v = jnp.zeros((ROWS_IMG, D), F32)
    for row in range(rows):
        here = slice(row * ROW, (row + 1) * ROW)
        d_out = do_ref[0, here, :]
        d_out_o = d_out * o_ref[0, here, :]
        q_t = (q_ref[0, here, :] * scale).T
        d_out_t = d_out.T
        v_t = jnp.concatenate([v_ref[0, here, :], sum_v], 0).T
        d_keys = []
        d_values = []
        for pair in range(PAIRS):
            lanes = slice(pair * PAIR, (pair + 1) * PAIR)
            keys = jnp.concatenate([k_ref[0, here, lanes], sum_k[:, lanes]], 0)
            left = jnp.concatenate([d_out[:, lanes], d_out_o[:, lanes]], 1)
            d_query = None
            for half in range(2):
                head = 2 * pair + half
                mine = slice(head * HD, (head + 1) * HD)
                own = v_t[mine]
                right = [own, blank, minus, blank] if half == 0 else [blank, own, blank, minus]
                weight = e_ref[0, row, head]
                d_score = weight * dot(left, jnp.concatenate(right, 0)).astype(BF16)
                d_values.append(dot(d_out_t[mine], weight).astype(BF16))
                d_keys.append(dot(q_t[mine], d_score).astype(BF16))
                part = dot(d_score, keys * masks[half])
                d_query = part if d_query is None else d_query + part
            grad_ref[0, here, lanes] = (d_query * scale).astype(BF16)
        d_key = jnp.concatenate(d_keys, 0).T
        d_value = jnp.concatenate(d_values, 0).T
        grad_ref[0, here, D : 2 * D] = d_key[:ROW]
        grad_ref[0, here, 2 * D :] = d_value[:ROW]
        d_sum_k += d_key[ROW:].astype(F32)
        d_sum_v += d_value[ROW:].astype(F32)
    dsk_ref[step] = d_sum_k.astype(BF16)
    dsv_ref[step] = d_sum_v.astype(BF16)
    acc_ref[...] += dot(with_ones(xh_ref[0].T), grad_ref[0])

    @pl.when(step == pl.num_programs(0) - 1)
    def _():
        mean_t = with_ones(mean_ref[...].reshape(-1, D).T)
        all_k = dsk_ref[...].reshape(-1, D)
        all_v = dsv_ref[...].reshape(-1, D)
        acc_ref[:, D : 2 * D] += dot(mean_t, all_k)
        acc_ref[:, 2 * D :] += dot(mean_t, all_v)
        d_mean = dot_nt(all_k, weights[1][0]) + dot_nt(all_v, weights[2][0])
        dm_ref[...] = d_mean.astype(BF16).reshape(dm_ref.shape)
        gain_grad = jnp.zeros((D, 1), F32)
        shift_grad = jnp.zeros((1, D), F32)
        gain = jnp.broadcast_to(params_ref[:, 0:D], (8, D)).T[:, 0:1]
        shift = jnp.broadcast_to(params_ref[:, D : 2 * D], (8, D)).T[:, 0:1]
        for block, w_ref in enumerate(weights):
            columns = slice(block * D, (block + 1) * D)
            product = acc_ref[0:D, columns]
            sums = acc_ref[D : D + 1, columns]
            gain_grad += jnp.sum(product * w_ref[0].astype(F32), -1, keepdims=True)
            high = sums.astype(BF16)
            parts = jnp.concatenate([high, (sums - high.astype(F32)).astype(BF16)], 0)
            parts = jnp.concatenate([parts, jnp.zeros((14, D), BF16)], 0)
            shift_grad += jnp.sum(dot_nt(parts, w_ref[0]), 0, keepdims=True)
            acc_ref[0:D, columns] = product * gain + shift * sums
        small_ref[:, 0:D] = jnp.broadcast_to(gain_grad, (D, 128)).T[0:1]
        small_ref[:, D:] = shift_grad
        if pieces:
            write_pieces(place, grads_refs, lambda block, here: acc_ref[here, block * D : (block + 1) * D])
        else:
            for block in range(3):
                grads_refs[0][block] = acc_ref[0:D, block * D : (block + 1) * D].astype(BF16)


def back_call(owner, place, groups, operands, params, slots):
    images, count, _ = operands[0].shape
    rows = count // ROW
    grads = grad_shapes(groups, 3, groups and group_sizes(groups[1]))
    return pl.pallas_call(
        functools.partial(back_kernel, groups is not None),
        grid_spec=pltpu.PrefetchScalarGridSpec(
            num_scalar_prefetch=2,
            grid=(images,),
            in_specs=[tile_spec(count, D)] * 5
            + [tile_spec(rows, HEADS, ROW, KEYS), tile_spec(count, D)]
            + [tile_spec(ROWS_IMG, D)] * 2
            + [whole_spec((images, ROWS_IMG, D)), whole_spec(params.shape)]
            + [weight_spec(block) for block in range(3)],
            out_specs=[tile_spec(count, 3 * D), out_whole((images, ROWS_IMG, D)), out_whole((1, 2 * D))]
            + [out_whole(shape) for shape in grads],
            scratch_shapes=[
                pltpu.VMEM((D + 16, 3 * D), F32),
                pltpu.VMEM((images, ROWS_IMG, D), BF16),
                pltpu.VMEM((images, ROWS_IMG, D), BF16),
            ],
        ),
        out_shape=[
            jax.ShapeDtypeStruct((images, count, 3 * D), BF16),
            jax.ShapeDtypeStruct((images, ROWS_IMG, D), BF16),
            jax.ShapeDtypeStruct((1, 2 * D), F32),
        ]
        + [jax.ShapeDtypeStruct(shape, BF16) for shape in grads],
        compiler_params=pltpu.CompilerParams(vmem_limit_bytes=60 * MIB),
        cost_estimate=pl.CostEstimate(
            flops=images * count * D * D * 20, bytes_accessed=images * count * D * 24, transcendentals=0
        ),
        name="attend_back",
    )(owner, place, *operands, params, slots, slots, slots)


def low_kernel(owner, grad_ref, wq_ref, wk_ref, wv_ref, low_ref):
    joined = jnp.concatenate([wq_ref[0], wk_ref[0], wv_ref[0]], 1)
    low_ref[...] = dot_nt(grad_ref[...].reshape(-1, 3 * D), joined).astype(BF16).reshape(low_ref.shape)


def low_call(owner, grads, slots):
    images, count, _ = grads.shape
    return pl.pallas_call(
        low_kernel,
        grid_spec=pltpu.PrefetchScalarGridSpec(
            num_scalar_prefetch=1,
            grid=(images // 2,),
            in_specs=[two_spec(count, 3 * D)] + [weight_spec(block) for block in range(3)],
            out_specs=two_spec(count, D),
        ),
        out_shape=jax.ShapeDtypeStruct((images, count, D), BF16),
        compiler_params=pltpu.CompilerParams(vmem_limit_bytes=60 * MIB),
        cost_estimate=pl.CostEstimate(
            flops=images * count * D * D * 6, bytes_accessed=images * count * D * 8, transcendentals=0
        ),
        name="project_back",
    )(owner, grads, slots, slots, slots)


def last_kernel(xh_ref, scale_ref, low_ref, dr_ref, dm_ref, params_ref, out_ref):
    g_ref = params_ref.at[:, 0:D]
    for image, row in itertools.product(range(2), range(dm_ref.shape[1])):
        here = slice(row * ROW, (row + 1) * ROW)
        normal, spread = xh_ref[image, here, :].astype(F32), scale_ref[image, here, :]
        total = low_ref[image, here, :].astype(F32) + dm_ref[image, row : row + 1, :] * (1.0 / ROW)
        d_normal = total * g_ref[...]
        middle = jnp.mean(d_normal, -1, keepdims=True)
        along = jnp.mean(d_normal * normal, -1, keepdims=True)
        out_ref[image, here, :] = dr_ref[image, here, :].astype(F32) + spread * (d_normal - middle - normal * along)


def last_call(normal, scale, d_low, d_branch, d_mean, params):
    images, count, _ = normal.shape
    return pl.pallas_call(
        last_kernel,
        grid=(images // 2,),
        in_specs=[two_spec(count, D), two_spec(count, 1), two_spec(count, D), two_spec(count, D)]
        + [two_spec(count // ROW, D), whole_spec(params.shape)],
        out_specs=two_spec(count, D),
        out_shape=jax.ShapeDtypeStruct((images, count, D), F32),
        compiler_params=pltpu.CompilerParams(vmem_limit_bytes=60 * MIB),
        cost_estimate=pl.CostEstimate(
            flops=images * count * D * 20, bytes_accessed=images * count * D * 11, transcendentals=0
        ),
        name="norm_one_back",
    )(normal, scale, d_low, d_branch, d_mean, params)


def adamw_update(weight_now, gradient, first_moment, second_moment, decay_rate, step_rate):
    first_new = 0.9 * first_moment + 0.1 * gradient
    second_new = 0.95 * second_moment + 0.05 * gradient * gradient
    direction = first_new / (1.0 - 0.9**STEP) / (jnp.sqrt(second_new / (1.0 - 0.95**STEP)) + 1e-08)
    return (weight_now - step_rate * (direction + decay_rate * weight_now), first_new, second_new)


def swap(value, axis, bit):
    size = lax.axis_size(axis)
    return lax.ppermute(value, axis, [(index, index ^ bit) for index in range(size)])


def to_rows(values):
    high = lax.reduce_precision(values, 8, 7)
    rows = jnp.concatenate([high, values - high], 1).reshape(-1, D).astype(BF16)
    return jnp.pad(rows, ((0, -rows.shape[0] % 16), (0, 0)))


def from_rows(rows, size):
    count = size // D
    return (rows[:count] + rows[count : 2 * count]).reshape(1, size)


def join(value):
    inner, outer = group_sizes(lax.axis_size("wide"))
    far = jnp.stack([value] + [swap(value, "wide", inner * step) for step in range(1, outer)])
    near = jnp.stack([far] + [swap(far, "wide", step) for step in range(1, inner)], 1)
    return near.reshape((inner * outer,) + value.shape)


def reorder(value, axis, dim=0):
    return jnp.take(value, lax.axis_index(axis) ^ jnp.arange(lax.axis_size(axis)), axis=dim)


def fetch_blocks(low_master, owners, means, whole_pieces):
    wide = lax.axis_size("wide")
    narrow = lax.axis_size("narrow")
    pieces = lax.all_to_all(low_master.reshape(wide, -1, D), "wide", 0, 0, tiled=True)
    mine = jnp.take(pieces, owners, axis=0)
    count, depth, _ = mine.shape
    joined = join(jnp.concatenate([mine.reshape(-1, D), means.reshape(-1, D)], 0))
    mean_all = joined[:, count * depth :].reshape((wide,) + means.shape).swapaxes(0, 1)
    mean_all = mean_all.reshape(means.shape[0], -1, D)
    if whole_pieces:
        return [joined] + [swap(joined, "narrow", step) for step in range(1, narrow)], mean_all
    rows = joined[:, : count * depth]
    halves = jnp.stack([rows] + [swap(rows, "narrow", step) for step in range(1, narrow)])
    halves = reorder(reorder(halves, "narrow"), "wide", 1).reshape(narrow, wide, count, depth, D)
    return [halves.transpose(2, 0, 1, 3, 4).reshape(count, D, D)], mean_all


def piece_lists(grads):
    if len(grads) > 1:
        return list(grads)
    (blocks,) = grads
    narrow = lax.axis_size("narrow")
    wide = lax.axis_size("wide")
    parts = blocks.reshape(blocks.shape[0], narrow, wide, -1, D).transpose(1, 2, 0, 3, 4)
    return list(reorder(parts, "narrow").reshape(narrow, wide, -1, D))


def by_group(pieces):
    inner, outer = group_sizes(lax.axis_size("wide"))
    return pieces.reshape((outer, inner) + pieces.shape[1:]).swapaxes(0, 1)


def sum_narrow(lists):
    total = lists[0].astype(F32)
    for step in range(1, len(lists)):
        total += swap(lists[step], "narrow", step).astype(F32)
    return total.astype(BF16)


def sum_group(pieces, stride):
    total = pieces[0].astype(F32)
    for step in range(1, len(pieces)):
        total += swap(pieces[step], "wide", step * stride).astype(F32)
    return total


def per_device(
    tokens, cotangent, owner_list, master, moment_one, moment_two, small_params, small_one, small_two
):
    images, count, _ = tokens.shape
    rows = count // ROW
    wide = lax.axis_size("wide")
    small = small_params.reshape(1, -1)
    low_master = master.astype(BF16)
    slots = lax.all_gather(low_master.reshape(-1, D), ("wide", "narrow"), axis=0, tiled=True)
    slots = slots.reshape(-1, D, D)
    narrow = lax.axis_size("narrow")
    inner, outer = group_sizes(wide)
    depth = D // narrow // wide
    groups = (narrow, wide) if depth % 16 == 0 and narrow > 1 else None
    me = lax.axis_index("wide")
    names = owner_list[None, :] == jnp.arange(wide, dtype=jnp.int32)[:, None]
    owned = jnp.any(names, 1)
    block_of = jnp.argmax(names, 1)
    place = jnp.stack([me, lax.axis_index("narrow")]).astype(jnp.int32)
    place, small, owned, block_of, tokens = lax.optimization_barrier((place, small, owned, block_of, tokens))
    normal, scale, means = norm_call(tokens)
    parts, mean_all = fetch_blocks(low_master, owner_list[:3], means, groups is not None)
    queries, keys, values, weights, attended, inverse, sum_k, sum_v = attend_call(
        place, normal, mean_all, small, parts
    )
    block_out, d_branch, d_out, late_small, *grads_late = ff_call(
        owner_list, place, groups, tokens, attended, cotangent, inverse, small, slots
    )

    tie = lax.optimization_barrier
    late, queries = tie((sum_narrow(piece_lists(grads_late)), queries))
    late = lax.all_to_all(late, "wide", 0, 0, tiled=True)
    operands = (queries, keys, values, attended, d_out, weights, normal, sum_k, sum_v, mean_all)
    d_joined, d_mean, early_small, *grads_early = back_call(
        owner_list, place, groups, operands, small, slots
    )
    late, early_small, *grads_early = tie((late, early_small, *grads_early))
    late = jnp.sum(late.astype(F32), 0)
    small_sums = jnp.concatenate([early_small, late_small], 1)
    size = small_sums.shape[1]
    bit = 1
    while bit < narrow:
        small_sums = small_sums + swap(small_sums, "narrow", bit)
        bit *= 2
    d_mean = by_group(d_mean.reshape(images, wide, rows, D).swapaxes(0, 1).reshape(wide, -1, D))
    early = sum_narrow(piece_lists(grads_early))
    if groups is None:
        early = by_group(reorder(early, "wide"))
    early, small_sums, d_joined = tie((early, small_sums, d_joined))
    d_low = low_call(owner_list, d_joined, slots)

    cuts = (3 * depth, 3 * depth + images * rows)
    small_rows = to_rows(small_sums)
    near = jnp.concatenate([early, d_mean], 2).reshape(inner, outer * cuts[1], D)
    near = sum_group([jnp.concatenate([near[step], small_rows], 0) for step in range(inner)], 1)
    near, late, d_low = tie((near, late, d_low))
    small_rows = to_rows(from_rows(near[outer * cuts[1] :], size))
    far = near[: outer * cuts[1]].astype(BF16).reshape(outer, cuts[1], D)
    far = sum_group([jnp.concatenate([far[step], small_rows], 0) for step in range(outer)], inner)
    own_mean = far[cuts[0] : cuts[1]].reshape(images, rows, D)
    small_grad = from_rows(far[cuts[1] :], size).reshape(-1)
    shares = jnp.concatenate([far[: cuts[0]], late], 0).reshape(-1, depth, D).astype(BF16)

    moved = jnp.where(owned[:, None, None], jnp.take(shares, block_of, axis=0), jnp.zeros((), BF16))
    moved = lax.all_to_all(moved, "wide", 0, 0, tiled=True)
    grad_tokens = last_call(normal, scale, d_low, d_branch, own_mean, small)
    moved, grad_tokens = tie((moved, grad_tokens))
    own_grad = moved.reshape(1, -1, D).astype(F32)
    owns_slot = owned[me]
    slot_weight, slot_first, slot_second = adamw_update(
        master, own_grad, moment_one, moment_two, 0.1, RATE
    )
    new_master = jnp.where(owns_slot, slot_weight, master)
    new_one = jnp.where(owns_slot, slot_first, moment_one)
    new_two = jnp.where(owns_slot, slot_second, moment_two)
    small_new, small_one_new, small_two_new = adamw_update(
        small_params, small_grad, small_one, small_two, 0.0, GAIN_RATE
    )
    return (block_out, grad_tokens, new_master, new_one, new_two, small_new, small_one_new, small_two_new)


def solution(mesh):
    split = P("narrow", "wide", None)
    slot = P("wide", "narrow", None)
    return jax.shard_map(
        per_device,
        mesh=mesh,
        in_specs=(split, split, P(), slot, slot, slot, P(), P(), P()),
        out_specs=(split, split, slot, slot, slot, P(), P(), P()),
        check_vma=False,
    )
```

profile of v0, /device:TPU:0, one launch (start us, length us, event | category | flops | bytes accessed | tf_op | source)
XLA Modules:
  0.0 366.4 jit_solution(17375209679508714198)
XLA Ops:
  7.2 1.8 convert_element_type.82
  9.0 8.3 %all-to-all-start = ((bf16[16,16,512]{2,1,0:T(8,128)(2,1)}), bf16[16,16,512]{2,1,0:T(8,128)(2,1)S(1)}, u32[]{:S(2)}, u32[]{:S(2)}) async-start(bf16[16,16,512]{2,1,0:T(8,128)(2,1)} %bitcast.66), calls=%async_computation | async-start | bytes 524288 | tf_op jit(solution)/shard_map/all_to_all | solution.py:581
  17.4 1.3 iota_reduce_fusion
  18.7 0.6 pad_add_fusion.place
  19.3 1.3 reshape.147.params_ref.refs_10_
  20.6 1.3 fusion.20
  21.9 10.1 %norm_one.1 = (bf16[8,768,512]{2,1,0:T(8,128)(2,1)}, f32[8,768,1]{2,1,0:T(8,128)}, bf16[8,4,512]{2,1,0:T(4,128)(2,1)}) custom-call(bf16[8,768,512]{2,1,0:T(8,128)(2,1)} %x_ref.1), custom_call_target="tpu_custom_call" | custom-call | flops 31457280 | bytes 12582912 | tf_op jit(solution)/shard_map/norm_one/pallas_call | solution.py:94
  32.1 0.8 reshape.149
  33.0 0.6 gather_fusion
  33.7 3.8 %collective-permute-start.2 = (bf16[80,512]{1,0:T(8,128)(2,1)S(1)}, bf16[80,512]{1,0:T(8,128)(2,1)S(1)}, u32[]{:S(2)}, u32[]{:S(2)}) collective-permute-start(bf16[80,512]{1,0:T(8,128)(2,1)S(1)} %get-tuple-element.111), channel_id=1, source_target_pairs={{0,24},{2,26},{4,28},{6,30},{8,16},{10,18},{12,20},{14,22},{16,8},... | collective-permute-start | bytes 245768 | tf_op jit(solution)/shard_map/ppermute | solution.py:553
  37.5 0.6 collective-permute-start
  38.1 2.8 collective-permute-done.2
  40.9 5.8 %collective-permute-done.1 = bf16[80,512]{1,0:T(8,128)(2,1)S(1)} collective-permute-done((bf16[80,512]{1,0:T(8,128)(2,1)S(1)}, bf16[80,512]{1,0:T(8,128)(2,1)S(1)}, u32[]{:S(2)}, u32[]{:S(2)}) %collective-permute-start.1) | collective-permute-done | bytes 81952 | tf_op jit(solution)/shard_map/ppermute | solution.py:553
  46.8 2.5 collective-permute-start.5
  49.3 0.5 collective-permute-start.4
  49.8 0.6 collective-permute-start.3
  50.4 8.3 %collective-permute-done.5 = bf16[4,80,512]{2,1,0:T(8,128)(2,1)S(1)} collective-permute-done((bf16[4,80,512]{2,1,0:T(8,128)(2,1)S(1)}, bf16[4,80,512]{2,1,0:T(8,128)(2,1)S(1)}, u32[]{:S(2)}, u32[]{:S(2)}) %collective-permute-start.5) | collective-permute-done | bytes 327712 | tf_op jit(solution)/shard_map/ppermute | solution.py:553
  58.6 4.1 %collective-permute-done.4 = bf16[4,80,512]{2,1,0:T(8,128)(2,1)S(1)} collective-permute-done((bf16[4,80,512]{2,1,0:T(8,128)(2,1)S(1)}, bf16[4,80,512]{2,1,0:T(8,128)(2,1)S(1)}, u32[]{:S(2)}, u32[]{:S(2)}) %collective-permute-start.4) | collective-permute-done | bytes 327712 | tf_op jit(solution)/shard_map/ppermute | solution.py:553
  62.7 0.9 collective-permute-done.3
  64.3 0.9 reshape.152.mean_ref.refs_9_
  65.2 3.7 %collective-permute-done.6.refs_1_ = bf16[16,80,512]{2,1,0:T(8,128)(2,1)} collective-permute-done((bf16[16,80,512]{2,1,0:T(8,128)(2,1)S(1)}, bf16[16,80,512]{2,1,0:T(8,128)(2,1)}, u32[]{:S(2)}, u32[]{:S(2)}) %collective-permute-start.6) | collective-permute-done | bytes 1310752 | tf_op jit(solution)/shard_map/ppermute | solution.py:553
  69.0 34.4 %attend.1 = (bf16[8,768,512]{2,1,0:T(8,128)(2,1)}, bf16[8,768,512]{2,1,0:T(8,128)(2,1)}, bf16[8,768,512]{2,1,0:T(8,128)(2,1)}, bf16[8,4,8,192,256]{4,3,2,1,0:T(8...) custom-call(s32[2]{0:T(128)} %pad_add_fusion.place, ...), custom_call_target="tpu_custom_call" | custom-call | flops 16106127360 | bytes 62914560 | tf_op jit(solution)/shard_map/attend/pallas_call | solution.py:208
  103.4 116.4 %feed_forward.1 = (bf16[8,768,512]{2,1,0:T(8,128)(2,1)}, bf16[8,768,512]{2,1,0:T(8,128)(2,1)}, bf16[8,768,512]{2,1,0:T(8,128)(2,1)}, f32[1,3584]{1,0:T(1,128)}, ...) custom-call(s32[12]{0:T(128)} %owner.5, s32[2]{0:T(128)} %pad_add_fusion.place, bf16[8,768,512]{2,1,0:T(8,128)(2,1)} %x_ref.1, ...), custom_call_target="tpu_custom_call" | custom-call | flops 86973087744 | bytes 44040192 | tf_op jit(solution)/shard_map/feed_forward/pallas_call | solution.py:337
  220.0 4.6 %collective-permute-done.7 = bf16[16,144,512]{2,1,0:T(8,128)(2,1)S(1)} collective-permute-done((bf16[16,144,512]{2,1,0:T(8,128)(2,1)}, bf16[16,144,512]{2,1,0:T(8,128)(2,1)S(1)}, u32[]{:S(2)}, u32[]{:S(2)}) %collective-permute-start.7) | collective-permute-done | bytes 2359328 | tf_op jit(solution)/shard_map/ppermute | solution.py:553
  224.6 3.8 %add_convert_fusion = bf16[16,144,512]{2,1,0:T(8,128)(2,1)} fusion(bf16[16,144,512]{2,1,0:T(8,128)(2,1)S(1)} %collective-permute-done.7, bf16[16,144,512]{2,1,0:T(8,128)(2,1)} %get-tuple-element.61), kind=kLoop, calls=%fused_computation.3 | loop fusion | flops 4718592 | bytes 7077888 | tf_op jit(solution)/shard_map/convert_element_type | solution.py:614
  228.4 5.5 %all-to-all-start.1 = ((bf16[16,144,512]{2,1,0:T(8,128)(2,1)}), bf16[16,144,512]{2,1,0:T(8,128)(2,1)S(1)}, u32[]{:S(2)}, u32[]{:S(2)}) async-start(bf16[16,144,512]{2,1,0:T(8,128)(2,1)} %add_convert_fusion), calls=%async_computation.1 | async-start | bytes 4718592 | tf_op jit(solution)/shard_map/all_to_all | solution.py:655
  234.0 60.9 %attend_back.1 = (bf16[8,768,1536]{2,1,0:T(8,128)(2,1)}, bf16[8,64,512]{2,1,0:T(8,128)(2,1)}, f32[1,1024]{1,0:T(1,128)}, bf16[4,4,48,512]{3,2,1,0:T(8,128)(2,1)}, bf16[4,4,48,512]{3,2,1,0:T(8,128)(2,1)}) custom-call(s32[12]{0:T(128)} %owner.5, s32[2]{0:T(128)} %pad_add_fusion.place, bf16[8,768,512]{2,1,0:T(8,128)(2,1)} %get-tuple-element.65.refs_0_, ...), custom_call_target="tpu_custom_call" | custom-call | flops 32212254720 | bytes 75497472 | tf_op jit(solution)/shard_map/attend_back/pallas_call | solution.py:459
  294.9 1.2 reshape.155
  296.6 0.5 collective-permute-start.9
  297.2 0.3 convert_reduce_fusion
  297.5 1.4 collective-permute-done.9
  299.1 0.2 add_convert_fusion.1
  299.7 2.9 collective-permute-start.12
  302.6 0.6 collective-permute-start.11
  303.3 15.6 %project_back.1.low_ref = bf16[8,768,512]{2,1,0:T(8,128)(2,1)} custom-call(s32[12]{0:T(128)} %owner.5, bf16[8,768,1536]{2,1,0:T(8,128)(2,1)} %get-tuple-element.84.grad_ref, bf16[16,512,512]{2,1,0:T(8,128)(2,1)} %bitcast.60, bf16[16,512,512]{2,1,0:T(8,128)(2,1)} %bitcast.61, bf16[16,512,512]{2,1,0:T(8,128)(2,1)} %bitcast.62), custom_call_target="tpu_custom_call" | custom-call | flops 9663676416 | bytes 25165824 | tf_op jit(solution)/shard_map/project_back/pallas_call | solution.py:498
  319.1 0.3 collective-permute-done.10
  319.9 3.4 collective-permute-start.15
  323.3 1.1 collective-permute-start.13
  324.4 3.3 collective-permute-done.15
  327.7 5.6 %collective-permute-done.14 = bf16[112,512]{1,0:T(8,128)(2,1)S(1)} collective-permute-done((bf16[112,512]{1,0:T(8,128)(2,1)S(1)}, bf16[112,512]{1,0:T(8,128)(2,1)S(1)}, u32[]{:S(2)}, u32[]{:S(2)}) %collective-permute-start.14) | collective-permute-done | bytes 114720 | tf_op jit(solution)/shard_map/ppermute | solution.py:553
  333.4 0.6 gather_fusion.1
  334.0 0.8 select_select_fusion
  334.8 4.9 %all-to-all-start.2 = ((bf16[16,16,512]{2,1,0:T(8,128)(2,1)}), bf16[16,16,512]{2,1,0:T(8,128)(2,1)S(1)}, u32[]{:S(2)}, u32[]{:S(2)}) async-start(bf16[16,16,512]{2,1,0:T(8,128)(2,1)} %select_select_fusion), calls=%async_computation.2 | async-start | bytes 524288 | tf_op jit(solution)/shard_map/all_to_all | solution.py:688
  339.7 0.6 dynamic_slice.3
  340.3 0.7 reshape.157.dm_ref
  341.1 15.2 %norm_one_back.1 = f32[8,768,512]{2,1,0:T(8,128)} custom-call(bf16[8,768,512]{2,1,0:T(8,128)(2,1)} %get-tuple-element.53.xh_ref.refs_6_, f32[8,768,1]{2,1,0:T(8,128)} %get-tuple-element.87.scale_ref, bf16[8,768,512]{2,1,0:T(8,128)(2,1)} %project_back.1.low_ref, bf16[8,768,512]{2,1,0:T(8,128)(2,1)} %get-tuple-element.89.dr_ref, ...), custom_call_target="tpu_custom_call" | custom-call | flops 62914560 | bytes 34603008 | tf_op jit(solution)/shard_map/norm_one_back/pallas_call | solution.py:529
  356.3 0.6 multiply_subtract_fusion
  356.9 2.4 fusion.3
  (81 shorter events, 3.1 us)
Async XLA Ops:
  7.2 96.2 %all-gather.3.cloned.1.call-start = ((), (), s32[]{:S(2)}) async-start(), calls=%async_computation.3 | async-start | bytes 8650752 | tf_op jit(solution)/shard_map/all_gather | solution.py:632
  9.0 24.0 %all-to-all-start = ((bf16[16,16,512]{2,1,0:T(8,128)(2,1)}), bf16[16,16,512]{2,1,0:T(8,128)(2,1)S(1)}, u32[]{:S(2)}, u32[]{:S(2)}) async-start(bf16[16,16,512]{2,1,0:T(8,128)(2,1)} %bitcast.66), calls=%async_computation | async-start | bytes 524288 | tf_op jit(solution)/shard_map/all_to_all | solution.py:581
  21.9 10.9 %copy-start.10 = (s32[12]{0:T(128)S(1)}, s32[12]{0:T(128)}, u32[]{:S(2)}) copy-start(s32[12]{0:T(128)} %owner.5) | copy-start | bytes 148
  33.7 7.2 %collective-permute-start.2 = (bf16[80,512]{1,0:T(8,128)(2,1)S(1)}, bf16[80,512]{1,0:T(8,128)(2,1)S(1)}, u32[]{:S(2)}, u32[]{:S(2)}) collective-permute-start(bf16[80,512]{1,0:T(8,128)(2,1)S(1)} %get-tuple-element.111), channel_id=1, source_target_pairs={{0,24},{2,26},{4,28},{6,30},{8,16},{10,18},{12,20},{14,22},{16,8},... | collective-permute-start | bytes 245768 | tf_op jit(solution)/shard_map/ppermute | solution.py:553
  37.5 9.2 %collective-permute-start.1 = (bf16[80,512]{1,0:T(8,128)(2,1)S(1)}, bf16[80,512]{1,0:T(8,128)(2,1)S(1)}, u32[]{:S(2)}, u32[]{:S(2)}) collective-permute-start(bf16[80,512]{1,0:T(8,128)(2,1)S(1)} %get-tuple-element.111), channel_id=1, source_target_pairs={{0,16},{2,18},{4,20},{6,22},{8,24},{10,26},{12,28},{14,30},{16,0},... | collective-permute-start | bytes 245768 | tf_op jit(solution)/shard_map/ppermute | solution.py:553
  37.5 9.2 %collective-permute-start = (bf16[80,512]{1,0:T(8,128)(2,1)S(1)}, bf16[80,512]{1,0:T(8,128)(2,1)S(1)}, u32[]{:S(2)}, u32[]{:S(2)}) collective-permute-start(bf16[80,512]{1,0:T(8,128)(2,1)S(1)} %get-tuple-element.111), channel_id=1, source_target_pairs={{0,8},{2,10},{4,12},{6,14},{8,0},{10,2},{12,4},{14,6},{16,24},{18,... | collective-permute-start | bytes 245768 | tf_op jit(solution)/shard_map/ppermute | solution.py:553
  46.8 11.9 %collective-permute-start.5 = (bf16[4,80,512]{2,1,0:T(8,128)(2,1)S(1)}, bf16[4,80,512]{2,1,0:T(8,128)(2,1)S(1)}, u32[]{:S(2)}, u32[]{:S(2)}) collective-permute-start(bf16[4,80,512]{2,1,0:T(8,128)(2,1)S(1)} %get-tuple-element.109), channel_id=1, source_target_pairs={{0,6},{2,4},{4,2},{6,0},{8,14},{10,12},{12,10},{14,8},{16,22},{18,... | collective-permute-start | bytes 983048 | tf_op jit(solution)/shard_map/ppermute | solution.py:553
  49.3 13.4 %collective-permute-start.4 = (bf16[4,80,512]{2,1,0:T(8,128)(2,1)S(1)}, bf16[4,80,512]{2,1,0:T(8,128)(2,1)S(1)}, u32[]{:S(2)}, u32[]{:S(2)}) collective-permute-start(bf16[4,80,512]{2,1,0:T(8,128)(2,1)S(1)} %get-tuple-element.109), channel_id=1, source_target_pairs={{0,4},{2,6},{4,0},{6,2},{8,12},{10,14},{12,8},{14,10},{16,20},{18,... | collective-permute-start | bytes 983048 | tf_op jit(solution)/shard_map/ppermute | solution.py:553
  49.8 13.9 %collective-permute-start.3 = (bf16[4,80,512]{2,1,0:T(8,128)(2,1)S(1)}, bf16[4,80,512]{2,1,0:T(8,128)(2,1)S(1)}, u32[]{:S(2)}, u32[]{:S(2)}) collective-permute-start(bf16[4,80,512]{2,1,0:T(8,128)(2,1)S(1)} %get-tuple-element.109), channel_id=1, source_target_pairs={{0,2},{2,0},{4,6},{6,4},{8,10},{10,8},{12,14},{14,12},{16,18},{18,... | collective-permute-start | bytes 983048 | tf_op jit(solution)/shard_map/ppermute | solution.py:553
  63.8 5.1 %copy-start = (bf16[4,4,80,512]{3,2,1,0:T(8,128)(2,1)}, bf16[4,4,80,512]{3,2,1,0:T(8,128)(2,1)S(1)}, u32[]{:S(2)}) copy-start(bf16[4,4,80,512]{3,2,1,0:T(8,128)(2,1)S(1)} %pad_maximum_fusion) | copy-start | bytes 3932164
  63.8 5.1 %collective-permute-start.6 = (bf16[16,80,512]{2,1,0:T(8,128)(2,1)S(1)}, bf16[16,80,512]{2,1,0:T(8,128)(2,1)}, u32[]{:S(2)}, u32[]{:S(2)}) collective-permute-start(bf16[16,80,512]{2,1,0:T(8,128)(2,1)S(1)} %bitcast.63), channel_id=1, source_target_pairs={{0,1},{1,0},{2,3},{3,2},{4,5},{5,4},{6,7},{7,6},{8,9},{9,8},{10,11... | collective-permute-start | bytes 3932168 | tf_op jit(solution)/shard_map/ppermute | solution.py:553
  219.8 4.8 %collective-permute-start.7 = (bf16[16,144,512]{2,1,0:T(8,128)(2,1)}, bf16[16,144,512]{2,1,0:T(8,128)(2,1)S(1)}, u32[]{:S(2)}, u32[]{:S(2)}) collective-permute-start(bf16[16,144,512]{2,1,0:T(8,128)(2,1)} %get-tuple-element.62), channel_id=1, source_target_pairs={{0,1},{1,0},{2,3},{3,2},{4,5},{5,4},{6,7},{7,6},{8,9},{9,8},{10,11... | collective-permute-start | bytes 7077896 | tf_op jit(solution)/shard_map/ppermute | solution.py:553
  228.4 68.1 %all-to-all-start.1 = ((bf16[16,144,512]{2,1,0:T(8,128)(2,1)}), bf16[16,144,512]{2,1,0:T(8,128)(2,1)S(1)}, u32[]{:S(2)}, u32[]{:S(2)}) async-start(bf16[16,144,512]{2,1,0:T(8,128)(2,1)} %add_convert_fusion), calls=%async_computation.1 | async-start | bytes 4718592 | tf_op jit(solution)/shard_map/all_to_all | solution.py:655
  294.9 1.7 copy-start.9
  294.9 1.7 copy-start.8
  296.5 2.6 copy-start.2
  296.5 2.6 collective-permute-start.8
  296.6 2.3 collective-permute-start.9
  299.7 19.2 %collective-permute-start.12 = (bf16[352,512]{1,0:T(8,128)(2,1)S(1)}, bf16[352,512]{1,0:T(8,128)(2,1)S(1)}, u32[]{:S(2)}, u32[]{:S(2)}) collective-permute-start(bf16[352,512]{1,0:T(8,128)(2,1)S(1)} %get-tuple-element.117), channel_id=1, source_target_pairs={{0,6},{2,4},{4,2},{6,0},{8,14},{10,12},{12,10},{14,8},{16,22},{18,... | collective-permute-start | bytes 1081352 | tf_op jit(solution)/shard_map/ppermute | solution.py:553
  302.6 16.4 %collective-permute-start.11 = (bf16[352,512]{1,0:T(8,128)(2,1)S(1)}, bf16[352,512]{1,0:T(8,128)(2,1)S(1)}, u32[]{:S(2)}, u32[]{:S(2)}) collective-permute-start(bf16[352,512]{1,0:T(8,128)(2,1)S(1)} %get-tuple-element.116), channel_id=1, source_target_pairs={{0,4},{2,6},{4,0},{6,2},{8,12},{10,14},{12,8},{14,10},{16,20},{18,... | collective-permute-start | bytes 1081352 | tf_op jit(solution)/shard_map/ppermute | solution.py:553
  303.2 16.2 %collective-permute-start.10 = (bf16[352,512]{1,0:T(8,128)(2,1)S(1)}, bf16[352,512]{1,0:T(8,128)(2,1)S(1)}, u32[]{:S(2)}, u32[]{:S(2)}) collective-permute-start(bf16[352,512]{1,0:T(8,128)(2,1)S(1)} %get-tuple-element.115), channel_id=1, source_target_pairs={{0,2},{2,0},{4,6},{6,4},{8,10},{10,8},{12,14},{14,12},{16,18},{18,... | collective-permute-start | bytes 1081352 | tf_op jit(solution)/shard_map/ppermute | solution.py:553
  319.6 14.4 %copy-start.11 = (pred[16]{0:T(512)(128)(4,1)S(1)}, pred[16]{0:T(512)(128)(4,1)}, u32[]{:S(2)}) copy-start(pred[16]{0:T(512)(128)(4,1)} %fusion.20) | copy-start | bytes 52
  319.9 7.8 %collective-permute-start.15 = (bf16[112,512]{1,0:T(8,128)(2,1)S(1)}, bf16[112,512]{1,0:T(8,128)(2,1)S(1)}, u32[]{:S(2)}, u32[]{:S(2)}) collective-permute-start(bf16[112,512]{1,0:T(8,128)(2,1)S(1)} %get-tuple-element.114), channel_id=1, source_target_pairs={{0,24},{2,26},{4,28},{6,30},{8,16},{10,18},{12,20},{14,22},{16,8},... | collective-permute-start | bytes 344072 | tf_op jit(solution)/shard_map/ppermute | solution.py:553
  323.3 10.0 %collective-permute-start.14 = (bf16[112,512]{1,0:T(8,128)(2,1)S(1)}, bf16[112,512]{1,0:T(8,128)(2,1)S(1)}, u32[]{:S(2)}, u32[]{:S(2)}) collective-permute-start(bf16[112,512]{1,0:T(8,128)(2,1)S(1)} %get-tuple-element.113), channel_id=1, source_target_pairs={{0,16},{2,18},{4,20},{6,22},{8,24},{10,26},{12,28},{14,30},{16,0},... | collective-permute-start | bytes 344072 | tf_op jit(solution)/shard_map/ppermute | solution.py:553
  323.3 10.0 %collective-permute-start.13 = (bf16[112,512]{1,0:T(8,128)(2,1)S(1)}, bf16[112,512]{1,0:T(8,128)(2,1)S(1)}, u32[]{:S(2)}, u32[]{:S(2)}) collective-permute-start(bf16[112,512]{1,0:T(8,128)(2,1)S(1)} %get-tuple-element.112), channel_id=1, source_target_pairs={{0,8},{2,10},{4,12},{6,14},{8,0},{10,2},{12,4},{14,6},{16,24},{18,... | collective-permute-start | bytes 344072 | tf_op jit(solution)/shard_map/ppermute | solution.py:553
  334.8 22.1 %all-to-all-start.2 = ((bf16[16,16,512]{2,1,0:T(8,128)(2,1)}), bf16[16,16,512]{2,1,0:T(8,128)(2,1)S(1)}, u32[]{:S(2)}, u32[]{:S(2)}) async-start(bf16[16,16,512]{2,1,0:T(8,128)(2,1)} %select_select_fusion), calls=%async_computation.2 | async-start | bytes 524288 | tf_op jit(solution)/shard_map/all_to_all | solution.py:688
  341.0 15.3 %copy-start.5 = (f32[4608]{0:T(1024)S(1)}, f32[4608]{0:T(1024)}, u32[]{:S(2)}) copy-start(f32[4608]{0:T(1024)} %param.15) | copy-start | bytes 55300
  341.0 15.2 %copy-start.6 = (f32[4608]{0:T(1024)S(1)}, f32[4608]{0:T(1024)}, u32[]{:S(2)}) copy-start(f32[4608]{0:T(1024)} %param.16) | copy-start | bytes 55300
  341.0 15.2 %copy-start.7 = (f32[4608]{0:T(1024)S(1)}, f32[4608]{0:T(1024)}, u32[]{:S(2)}) copy-start(f32[4608]{0:T(1024)} %param.17) | copy-start | bytes 55300
  341.0 15.9 %copy-start.1 = (f32[1,256,512]{2,1,0:T(8,128)S(1)}, f32[1,256,512]{2,1,0:T(8,128)}, u32[]{:S(2)}) copy-start(f32[1,256,512]{2,1,0:T(8,128)} %param.12) | copy-start | bytes 1572868
  341.0 15.9 %copy-start.3 = (f32[1,256,512]{2,1,0:T(8,128)S(1)}, f32[1,256,512]{2,1,0:T(8,128)}, u32[]{:S(2)}) copy-start(f32[1,256,512]{2,1,0:T(8,128)} %param.14) | copy-start | bytes 1572868
  341.0 15.9 %copy-start.4 = (f32[1,256,512]{2,1,0:T(8,128)S(1)}, f32[1,256,512]{2,1,0:T(8,128)}, u32[]{:S(2)}) copy-start(f32[1,256,512]{2,1,0:T(8,128)} %param.13) | copy-start | bytes 1572868
Sparse Core Ops, SparseCore 0:
  10.9 83.2 all-gather.2
where the time goes:
time: 368 us; the launch traced here: 366 us
  Pallas kernels  253 us (69%)
  waiting for transfers between devices  41.2 us (11%)
  starting transfers between devices  35.6 us (10%)
  between operations  14.7 us (4%)
  other arithmetic  14.4 us (4%)
  local copies, waits for them, and re-layouts  7.72 us (2%)
    pallas_call x1, Pallas kernels, ff_call(): pl.pallas_call(functools.partial(ff_kernel, groups is not None), grid_spe...  116 us
    pallas_call x1, Pallas kernels, back_call(): pl.pallas_call(functools.partial(back_kernel, groups is not None), grid_s...  60.9 us
    ppermute x16, waiting for transfers between devices, swap(): lax.ppermute(value, axis, [(index, index ^ bit) for index in range(size)])  41.2 us
    pallas_call x1, Pallas kernels, attend_call(): pl.pallas_call(functools.partial(attend_kernel, len(parts)), grid_spec=pl...  34.4 us
    ppermute x16, starting transfers between devices, swap(): lax.ppermute(value, axis, [(index, index ^ bit) for index in range(size)])  16.9 us
    pallas_call x1, Pallas kernels, low_call(): pl.pallas_call(low_kernel, grid_spec=pltpu.PrefetchScalarGridSpec(num_sca...  15.6 us
    pallas_call x1, Pallas kernels, last_call(): pl.pallas_call(last_kernel, grid=(images // 2,), in_specs=[two_spec(count...  15.2 us
    pallas_call x1, Pallas kernels, norm_call(): pl.pallas_call(norm_kernel, grid=(images,), in_specs=[tile_spec(count, D)...  10.1 us
  transfers between devices with their start and end apart: 20, of which 13 were waited for; matrix products, arithmetic and copies ran while one was open for 3% of the time, Pallas kernels for 37%

commit v1 on v0

--- a/solution.py
+++ b/solution.py
@@ -428,7 +428,11 @@
         acc_ref[:, D : 2 * D] += dot(mean_t, all_k)
         acc_ref[:, 2 * D :] += dot(mean_t, all_v)
         d_mean = dot_nt(all_k, weights[1][0]) + dot_nt(all_v, weights[2][0])
-        dm_ref[...] = d_mean.astype(BF16).reshape(dm_ref.shape)
+        inner, outer, height, _ = dm_ref.shape
+        for distance in range(inner * outer):
+            first = range(distance * rows, d_mean.shape[0], ROWS_IMG)
+            piece = jnp.concatenate([d_mean[row : row + rows] for row in first], 0)
+            dm_ref[distance % inner, distance // inner] = piece.astype(BF16)
         gain_grad = jnp.zeros((D, 1), F32)
         shift_grad = jnp.zeros((1, D), F32)
         gain = jnp.broadcast_to(params_ref[:, 0:D], (8, D)).T[:, 0:1]
@@ -456,6 +460,7 @@
     images, count, _ = operands[0].shape
     rows = count // ROW
     grads = grad_shapes(groups, 3, groups and group_sizes(groups[1]))
+    mean_shape = group_sizes(ROWS_IMG // rows) + (images * rows, D)
     return pl.pallas_call(
         functools.partial(back_kernel, groups is not None),
         grid_spec=pltpu.PrefetchScalarGridSpec(
@@ -466,7 +471,7 @@
             + [tile_spec(ROWS_IMG, D)] * 2
             + [whole_spec((images, ROWS_IMG, D)), whole_spec(params.shape)]
             + [weight_spec(block) for block in range(3)],
-            out_specs=[tile_spec(count, 3 * D), out_whole((images, ROWS_IMG, D)), out_whole((1, 2 * D))]
+            out_specs=[tile_spec(count, 3 * D), out_whole(mean_shape), out_whole((1, 2 * D))]
             + [out_whole(shape) for shape in grads],
             scratch_shapes=[
                 pltpu.VMEM((D + 16, 3 * D), F32),
@@ -476,7 +481,7 @@
         ),
         out_shape=[
             jax.ShapeDtypeStruct((images, count, 3 * D), BF16),
-            jax.ShapeDtypeStruct((images, ROWS_IMG, D), BF16),
+            jax.ShapeDtypeStruct(mean_shape, BF16),
             jax.ShapeDtypeStruct((1, 2 * D), F32),
         ]
         + [jax.ShapeDtypeStruct(shape, BF16) for shape in grads],
@@ -512,25 +517,26 @@
     )(owner, grads, slots, slots, slots)
 
 
-def last_kernel(xh_ref, scale_ref, low_ref, dr_ref, dm_ref, params_ref, out_ref):
+def last_kernel(start, rows, xh_ref, scale_ref, low_ref, dr_ref, sums_ref, params_ref, out_ref):
     g_ref = params_ref.at[:, 0:D]
-    for image, row in itertools.product(range(2), range(dm_ref.shape[1])):
+    for image, row in itertools.product(range(2), range(rows)):
+        mean_row = start + (2 * pl.program_id(0) + image) * rows + row
         here = slice(row * ROW, (row + 1) * ROW)
         normal, spread = xh_ref[image, here, :].astype(F32), scale_ref[image, here, :]
-        total = low_ref[image, here, :].astype(F32) + dm_ref[image, row : row + 1, :] * (1.0 / ROW)
+        total = low_ref[image, here, :].astype(F32) + sums_ref[pl.ds(mean_row, 1), :] * (1.0 / ROW)
         d_normal = total * g_ref[...]
         middle = jnp.mean(d_normal, -1, keepdims=True)
         along = jnp.mean(d_normal * normal, -1, keepdims=True)
         out_ref[image, here, :] = dr_ref[image, here, :].astype(F32) + spread * (d_normal - middle - normal * along)
 
 
-def last_call(normal, scale, d_low, d_branch, d_mean, params):
+def last_call(normal, scale, d_low, d_branch, sums, start, params):
     images, count, _ = normal.shape
     return pl.pallas_call(
-        last_kernel,
+        functools.partial(last_kernel, start, count // ROW),
         grid=(images // 2,),
         in_specs=[two_spec(count, D), two_spec(count, 1), two_spec(count, D), two_spec(count, D)]
-        + [two_spec(count // ROW, D), whole_spec(params.shape)],
+        + [whole_spec(sums.shape), whole_spec(params.shape)],
         out_specs=two_spec(count, D),
         out_shape=jax.ShapeDtypeStruct((images, count, D), F32),
         compiler_params=pltpu.CompilerParams(vmem_limit_bytes=60 * MIB),
@@ -538,7 +544,7 @@
             flops=images * count * D * 20, bytes_accessed=images * count * D * 11, transcendentals=0
         ),
         name="norm_one_back",
-    )(normal, scale, d_low, d_branch, d_mean, params)
+    )(normal, scale, d_low, d_branch, sums, params)
 
 
 def adamw_update(weight_now, gradient, first_moment, second_moment, decay_rate, step_rate):
@@ -665,7 +671,6 @@
     while bit < narrow:
         small_sums = small_sums + swap(small_sums, "narrow", bit)
         bit *= 2
-    d_mean = by_group(d_mean.reshape(images, wide, rows, D).swapaxes(0, 1).reshape(wide, -1, D))
     early = sum_narrow(piece_lists(grads_early))
     if groups is None:
         early = by_group(reorder(early, "wide"))
@@ -680,13 +685,12 @@
     small_rows = to_rows(from_rows(near[outer * cuts[1] :], size))
     far = near[: outer * cuts[1]].astype(BF16).reshape(outer, cuts[1], D)
     far = sum_group([jnp.concatenate([far[step], small_rows], 0) for step in range(outer)], inner)
-    own_mean = far[cuts[0] : cuts[1]].reshape(images, rows, D)
     small_grad = from_rows(far[cuts[1] :], size).reshape(-1)
     shares = jnp.concatenate([far[: cuts[0]], late], 0).reshape(-1, depth, D).astype(BF16)
 
     moved = jnp.where(owned[:, None, None], jnp.take(shares, block_of, axis=0), jnp.zeros((), BF16))
     moved = lax.all_to_all(moved, "wide", 0, 0, tiled=True)
-    grad_tokens = last_call(normal, scale, d_low, d_branch, own_mean, small)
+    grad_tokens = last_call(normal, scale, d_low, d_branch, far, cuts[0], small)
     moved, grad_tokens = tie((moved, grad_tokens))
     own_grad = moved.reshape(1, -1, D).astype(F32)
     owns_slot = owned[me]

time: 368 us -> 355 us (0.965)
  Pallas kernels: 253 us -> 243 us
    pallas_call x1, Pallas kernels: 116 us -> 107 us  [ff_call(): pl.pallas_call(functools.partial(ff_kernel, groups is not None), grid_spe...]
  transfers between devices with their start and end apart: 20 -> 20, of which waited for: 13 -> 13; matrix products, arithmetic and copies ran while one was open for 3% -> 3% of each run, Pallas kernels for 37% -> 38%
where the time goes in v1:
time: 355 us; the launch traced here: 354 us
  Pallas kernels  243 us (68%)
  waiting for transfers between devices  40.5 us (11%)
  starting transfers between devices  35.6 us (10%)
  between operations  14.5 us (4%)
  other arithmetic  14.3 us (4%)
  local copies, waits for them, and re-layouts  6.38 us (2%)
    pallas_call x1, Pallas kernels, ff_call(): pl.pallas_call(functools.partial(ff_kernel, groups is not None), grid_spe...  107 us
    pallas_call x1, Pallas kernels, back_call(): pl.pallas_call(functools.partial(back_kernel, groups is not None), grid_s...  60.9 us
    ppermute x16, waiting for transfers between devices, swap(): lax.ppermute(value, axis, [(index, index ^ bit) for index in range(size)])  40.5 us
    pallas_call x1, Pallas kernels, attend_call(): pl.pallas_call(functools.partial(attend_kernel, len(parts)), grid_spec=pl...  34.4 us
    ppermute x16, starting transfers between devices, swap(): lax.ppermute(value, axis, [(index, index ^ bit) for index in range(size)])  16.8 us
    pallas_call x1, Pallas kernels, low_call(): pl.pallas_call(low_kernel, grid_spec=pltpu.PrefetchScalarGridSpec(num_sca...  15.6 us
    pallas_call x1, Pallas kernels, last_call(): pl.pallas_call(functools.partial(last_kernel, start, count // ROW), grid=...  14.5 us
    pallas_call x1, Pallas kernels, norm_call(): pl.pallas_call(norm_kernel, grid=(images,), in_specs=[tile_spec(count, D)...  10.1 us
  transfers between devices with their start and end apart: 20, of which 13 were waited for; matrix products, arithmetic and copies ran while one was open for 3% of the time, Pallas kernels for 38%

profile of v1, /device:TPU:0, one launch (start us, length us, event | category | flops | bytes accessed | tf_op | source)
XLA Modules:
  0.0 354.1 jit_solution(8946978761484146748)
XLA Ops:
  7.2 1.8 convert_element_type.82
  9.0 8.3 %all-to-all-start = ((bf16[16,16,512]{2,1,0:T(8,128)(2,1)}), bf16[16,16,512]{2,1,0:T(8,128)(2,1)S(1)}, u32[]{:S(2)}, u32[]{:S(2)}) async-start(bf16[16,16,512]{2,1,0:T(8,128)(2,1)} %bitcast.60), calls=%async_computation | async-start | bytes 524288 | tf_op jit(solution)/shard_map/all_to_all | solution.py:587
  17.4 1.3 iota_reduce_fusion
  18.7 0.6 pad_add_fusion.place
  19.3 1.3 reshape.141.params_ref.refs_10_
  20.6 1.3 fusion.17
  22.0 10.1 %norm_one.1 = (bf16[8,768,512]{2,1,0:T(8,128)(2,1)}, f32[8,768,1]{2,1,0:T(8,128)}, bf16[8,4,512]{2,1,0:T(4,128)(2,1)}) custom-call(bf16[8,768,512]{2,1,0:T(8,128)(2,1)} %x_ref.1), custom_call_target="tpu_custom_call" | custom-call | flops 31457280 | bytes 12582912 | tf_op jit(solution)/shard_map/norm_one/pallas_call | solution.py:94
  32.1 0.8 reshape.143
  33.1 0.6 gather_fusion
  33.8 3.8 %collective-permute-start.2 = (bf16[80,512]{1,0:T(8,128)(2,1)S(1)}, bf16[80,512]{1,0:T(8,128)(2,1)S(1)}, u32[]{:S(2)}, u32[]{:S(2)}) collective-permute-start(bf16[80,512]{1,0:T(8,128)(2,1)S(1)} %get-tuple-element.111), channel_id=1, source_target_pairs={{0,24},{2,26},{4,28},{6,30},{8,16},{10,18},{12,20},{14,22},{16,8},... | collective-permute-start | bytes 245768 | tf_op jit(solution)/shard_map/ppermute | solution.py:559
  37.6 0.6 collective-permute-start
  38.2 2.8 collective-permute-done.2
  41.0 6.0 %collective-permute-done.1 = bf16[80,512]{1,0:T(8,128)(2,1)S(1)} collective-permute-done((bf16[80,512]{1,0:T(8,128)(2,1)S(1)}, bf16[80,512]{1,0:T(8,128)(2,1)S(1)}, u32[]{:S(2)}, u32[]{:S(2)}) %collective-permute-start.1) | collective-permute-done | bytes 81952 | tf_op jit(solution)/shard_map/ppermute | solution.py:559
  47.0 2.3 collective-permute-start.5
  49.4 0.6 collective-permute-start.4
  50.0 0.6 collective-permute-start.3
  50.6 8.0 %collective-permute-done.5 = bf16[4,80,512]{2,1,0:T(8,128)(2,1)S(1)} collective-permute-done((bf16[4,80,512]{2,1,0:T(8,128)(2,1)S(1)}, bf16[4,80,512]{2,1,0:T(8,128)(2,1)S(1)}, u32[]{:S(2)}, u32[]{:S(2)}) %collective-permute-start.5) | collective-permute-done | bytes 327712 | tf_op jit(solution)/shard_map/ppermute | solution.py:559
  58.6 4.5 %collective-permute-done.4 = bf16[4,80,512]{2,1,0:T(8,128)(2,1)S(1)} collective-permute-done((bf16[4,80,512]{2,1,0:T(8,128)(2,1)S(1)}, bf16[4,80,512]{2,1,0:T(8,128)(2,1)S(1)}, u32[]{:S(2)}, u32[]{:S(2)}) %collective-permute-start.4) | collective-permute-done | bytes 327712 | tf_op jit(solution)/shard_map/ppermute | solution.py:559
  63.1 0.6 collective-permute-done.3
  64.3 0.9 reshape.146.mean_ref.refs_9_
  65.2 3.7 %collective-permute-done.6.refs_1_ = bf16[16,80,512]{2,1,0:T(8,128)(2,1)} collective-permute-done((bf16[16,80,512]{2,1,0:T(8,128)(2,1)S(1)}, bf16[16,80,512]{2,1,0:T(8,128)(2,1)}, u32[]{:S(2)}, u32[]{:S(2)}) %collective-permute-start.6) | collective-permute-done | bytes 1310752 | tf_op jit(solution)/shard_map/ppermute | solution.py:559
  68.9 34.4 %attend.1 = (bf16[8,768,512]{2,1,0:T(8,128)(2,1)}, bf16[8,768,512]{2,1,0:T(8,128)(2,1)}, bf16[8,768,512]{2,1,0:T(8,128)(2,1)}, bf16[8,4,8,192,256]{4,3,2,1,0:T(8...) custom-call(s32[2]{0:T(128)} %pad_add_fusion.place, ...), custom_call_target="tpu_custom_call" | custom-call | flops 16106127360 | bytes 62914560 | tf_op jit(solution)/shard_map/attend/pallas_call | solution.py:208
  103.4 107.3 %feed_forward.1 = (bf16[8,768,512]{2,1,0:T(8,128)(2,1)}, bf16[8,768,512]{2,1,0:T(8,128)(2,1)}, bf16[8,768,512]{2,1,0:T(8,128)(2,1)}, f32[1,3584]{1,0:T(1,128)}, ...) custom-call(s32[12]{0:T(128)} %owner.5, s32[2]{0:T(128)} %pad_add_fusion.place, bf16[8,768,512]{2,1,0:T(8,128)(2,1)} %x_ref.1, ...), custom_call_target="tpu_custom_call" | custom-call | flops 86973087744 | bytes 44040192 | tf_op jit(solution)/shard_map/feed_forward/pallas_call | solution.py:337
  210.7 0.2 collective-permute-start.7
  210.8 4.6 %collective-permute-done.7 = bf16[16,144,512]{2,1,0:T(8,128)(2,1)S(1)} collective-permute-done((bf16[16,144,512]{2,1,0:T(8,128)(2,1)}, bf16[16,144,512]{2,1,0:T(8,128)(2,1)S(1)}, u32[]{:S(2)}, u32[]{:S(2)}) %collective-permute-start.7) | collective-permute-done | bytes 2359328 | tf_op jit(solution)/shard_map/ppermute | solution.py:559
  215.5 3.8 %add_convert_fusion = bf16[16,144,512]{2,1,0:T(8,128)(2,1)} fusion(bf16[16,144,512]{2,1,0:T(8,128)(2,1)S(1)} %collective-permute-done.7, bf16[16,144,512]{2,1,0:T(8,128)(2,1)} %get-tuple-element.61), kind=kLoop, calls=%fused_computation.3 | loop fusion | flops 4718592 | bytes 7077888 | tf_op jit(solution)/shard_map/convert_element_type | solution.py:620
  219.3 5.6 %all-to-all-start.1 = ((bf16[16,144,512]{2,1,0:T(8,128)(2,1)}), bf16[16,144,512]{2,1,0:T(8,128)(2,1)S(1)}, u32[]{:S(2)}, u32[]{:S(2)}) async-start(bf16[16,144,512]{2,1,0:T(8,128)(2,1)} %add_convert_fusion), calls=%async_computation.1 | async-start | bytes 4718592 | tf_op jit(solution)/shard_map/all_to_all | solution.py:661
  224.9 60.9 %attend_back.1 = (bf16[8,768,1536]{2,1,0:T(8,128)(2,1)}, bf16[4,4,32,512]{3,2,1,0:T(8,128)(2,1)}, f32[1,1024]{1,0:T(1,128)}, bf16[4,4,48,512]{3,2,1,0:T(8,128)(2,1)}, bf16[4,4,48,512]{3,2,1,0:T(8,128)(2,1)}) custom-call(s32[12]{0:T(128)} %owner.5, s32[2]{0:T(128)} %pad_add_fusion.place, bf16[8,768,512]{2,1,0:T(8,128)(2,1)} %get-tuple-element.65.refs_0_, ...), custom_call_target="tpu_custom_call" | custom-call | flops 32212254720 | bytes 75497472 | tf_op jit(solution)/shard_map/attend_back/pallas_call | solution.py:464
  285.9 0.7 constant_dynamic-update-slice_fusion.1
  286.6 0.4 collective-permute-start.9
  287.1 0.3 convert_reduce_fusion
  287.4 0.8 collective-permute-done.9
  288.3 0.2 add_convert_fusion.1
  289.1 2.9 collective-permute-start.12
  292.0 0.6 collective-permute-start.11
  292.6 15.6 %project_back.1.low_ref = bf16[8,768,512]{2,1,0:T(8,128)(2,1)} custom-call(s32[12]{0:T(128)} %owner.5, bf16[8,768,1536]{2,1,0:T(8,128)(2,1)} %get-tuple-element.84.grad_ref, bf16[16,512,512]{2,1,0:T(8,128)(2,1)} %bitcast.54, bf16[16,512,512]{2,1,0:T(8,128)(2,1)} %bitcast.55, bf16[16,512,512]{2,1,0:T(8,128)(2,1)} %bitcast.56), custom_call_target="tpu_custom_call" | custom-call | flops 9663676416 | bytes 25165824 | tf_op jit(solution)/shard_map/project_back/pallas_call | solution.py:503
  308.4 0.3 collective-permute-done.10
  309.3 3.4 collective-permute-start.15
  312.6 1.1 collective-permute-start.13
  313.7 3.3 collective-permute-done.15
  317.1 5.6 %collective-permute-done.14 = bf16[112,512]{1,0:T(8,128)(2,1)S(1)} collective-permute-done((bf16[112,512]{1,0:T(8,128)(2,1)S(1)}, bf16[112,512]{1,0:T(8,128)(2,1)S(1)}, u32[]{:S(2)}, u32[]{:S(2)}) %collective-permute-start.14) | collective-permute-done | bytes 114720 | tf_op jit(solution)/shard_map/ppermute | solution.py:559
  322.7 0.6 gather_fusion.1
  323.3 0.8 select_select_fusion
  324.1 4.9 %all-to-all-start.2 = ((bf16[16,16,512]{2,1,0:T(8,128)(2,1)}), bf16[16,16,512]{2,1,0:T(8,128)(2,1)S(1)}, u32[]{:S(2)}, u32[]{:S(2)}) async-start(bf16[16,16,512]{2,1,0:T(8,128)(2,1)} %select_select_fusion), calls=%async_computation.2 | async-start | bytes 524288 | tf_op jit(solution)/shard_map/all_to_all | solution.py:692
  329.0 0.6 dynamic_slice.3
  329.7 14.5 %norm_one_back.1 = f32[8,768,512]{2,1,0:T(8,128)} custom-call(bf16[8,768,512]{2,1,0:T(8,128)(2,1)} %get-tuple-element.53.xh_ref.refs_6_, f32[8,768,1]{2,1,0:T(8,128)} %get-tuple-element.87.scale_ref, bf16[8,768,512]{2,1,0:T(8,128)(2,1)} %project_back.1.low_ref, bf16[8,768,512]{2,1,0:T(8,128)(2,1)} %get-tuple-element.89.dr_ref, f32[112,512]{1,0:T(8,128)} %copy-done.2, ...), custom_call_target="tpu_custom_call" | custom-call | flops 62914560 | bytes 34603008 | tf_op jit(solution)/shard_map/norm_one_back/pallas_call | solution.py:535
  344.2 0.6 multiply_subtract_fusion
  344.9 2.4 fusion.3
  (79 shorter events, 2.6 us)
Async XLA Ops:
  7.2 96.2 %all-gather.3.cloned.1.call-start = ((), (), s32[]{:S(2)}) async-start(), calls=%async_computation.3 | async-start | bytes 8650752 | tf_op jit(solution)/shard_map/all_gather | solution.py:638
  9.0 24.1 %all-to-all-start = ((bf16[16,16,512]{2,1,0:T(8,128)(2,1)}), bf16[16,16,512]{2,1,0:T(8,128)(2,1)S(1)}, u32[]{:S(2)}, u32[]{:S(2)}) async-start(bf16[16,16,512]{2,1,0:T(8,128)(2,1)} %bitcast.60), calls=%async_computation | async-start | bytes 524288 | tf_op jit(solution)/shard_map/all_to_all | solution.py:587
  22.0 10.9 %copy-start.11 = (s32[12]{0:T(128)S(1)}, s32[12]{0:T(128)}, u32[]{:S(2)}) copy-start(s32[12]{0:T(128)} %owner.5) | copy-start | bytes 148
  33.8 7.2 %collective-permute-start.2 = (bf16[80,512]{1,0:T(8,128)(2,1)S(1)}, bf16[80,512]{1,0:T(8,128)(2,1)S(1)}, u32[]{:S(2)}, u32[]{:S(2)}) collective-permute-start(bf16[80,512]{1,0:T(8,128)(2,1)S(1)} %get-tuple-element.111), channel_id=1, source_target_pairs={{0,24},{2,26},{4,28},{6,30},{8,16},{10,18},{12,20},{14,22},{16,8},... | collective-permute-start | bytes 245768 | tf_op jit(solution)/shard_map/ppermute | solution.py:559
  37.6 9.4 %collective-permute-start.1 = (bf16[80,512]{1,0:T(8,128)(2,1)S(1)}, bf16[80,512]{1,0:T(8,128)(2,1)S(1)}, u32[]{:S(2)}, u32[]{:S(2)}) collective-permute-start(bf16[80,512]{1,0:T(8,128)(2,1)S(1)} %get-tuple-element.111), channel_id=1, source_target_pairs={{0,16},{2,18},{4,20},{6,22},{8,24},{10,26},{12,28},{14,30},{16,0},... | collective-permute-start | bytes 245768 | tf_op jit(solution)/shard_map/ppermute | solution.py:559
  37.6 9.4 %collective-permute-start = (bf16[80,512]{1,0:T(8,128)(2,1)S(1)}, bf16[80,512]{1,0:T(8,128)(2,1)S(1)}, u32[]{:S(2)}, u32[]{:S(2)}) collective-permute-start(bf16[80,512]{1,0:T(8,128)(2,1)S(1)} %get-tuple-element.111), channel_id=1, source_target_pairs={{0,8},{2,10},{4,12},{6,14},{8,0},{10,2},{12,4},{14,6},{16,24},{18,... | collective-permute-start | bytes 245768 | tf_op jit(solution)/shard_map/ppermute | solution.py:559
  47.0 11.6 %collective-permute-start.5 = (bf16[4,80,512]{2,1,0:T(8,128)(2,1)S(1)}, bf16[4,80,512]{2,1,0:T(8,128)(2,1)S(1)}, u32[]{:S(2)}, u32[]{:S(2)}) collective-permute-start(bf16[4,80,512]{2,1,0:T(8,128)(2,1)S(1)} %get-tuple-element.109), channel_id=1, source_target_pairs={{0,6},{2,4},{4,2},{6,0},{8,14},{10,12},{12,10},{14,8},{16,22},{18,... | collective-permute-start | bytes 983048 | tf_op jit(solution)/shard_map/ppermute | solution.py:559
  49.4 13.7 %collective-permute-start.4 = (bf16[4,80,512]{2,1,0:T(8,128)(2,1)S(1)}, bf16[4,80,512]{2,1,0:T(8,128)(2,1)S(1)}, u32[]{:S(2)}, u32[]{:S(2)}) collective-permute-start(bf16[4,80,512]{2,1,0:T(8,128)(2,1)S(1)} %get-tuple-element.109), channel_id=1, source_target_pairs={{0,4},{2,6},{4,0},{6,2},{8,12},{10,14},{12,8},{14,10},{16,20},{18,... | collective-permute-start | bytes 983048 | tf_op jit(solution)/shard_map/ppermute | solution.py:559
  50.0 13.7 %collective-permute-start.3 = (bf16[4,80,512]{2,1,0:T(8,128)(2,1)S(1)}, bf16[4,80,512]{2,1,0:T(8,128)(2,1)S(1)}, u32[]{:S(2)}, u32[]{:S(2)}) collective-permute-start(bf16[4,80,512]{2,1,0:T(8,128)(2,1)S(1)} %get-tuple-element.109), channel_id=1, source_target_pairs={{0,2},{2,0},{4,6},{6,4},{8,10},{10,8},{12,14},{14,12},{16,18},{18,... | collective-permute-start | bytes 983048 | tf_op jit(solution)/shard_map/ppermute | solution.py:559
  63.8 5.1 %copy-start = (bf16[4,4,80,512]{3,2,1,0:T(8,128)(2,1)}, bf16[4,4,80,512]{3,2,1,0:T(8,128)(2,1)S(1)}, u32[]{:S(2)}) copy-start(bf16[4,4,80,512]{3,2,1,0:T(8,128)(2,1)S(1)} %pad_maximum_fusion) | copy-start | bytes 3932164
  63.9 5.1 %collective-permute-start.6 = (bf16[16,80,512]{2,1,0:T(8,128)(2,1)S(1)}, bf16[16,80,512]{2,1,0:T(8,128)(2,1)}, u32[]{:S(2)}, u32[]{:S(2)}) collective-permute-start(bf16[16,80,512]{2,1,0:T(8,128)(2,1)S(1)} %bitcast.57), channel_id=1, source_target_pairs={{0,1},{1,0},{2,3},{3,2},{4,5},{5,4},{6,7},{7,6},{8,9},{9,8},{10,11... | collective-permute-start | bytes 3932168 | tf_op jit(solution)/shard_map/ppermute | solution.py:559
  210.7 4.8 %collective-permute-start.7 = (bf16[16,144,512]{2,1,0:T(8,128)(2,1)}, bf16[16,144,512]{2,1,0:T(8,128)(2,1)S(1)}, u32[]{:S(2)}, u32[]{:S(2)}) collective-permute-start(bf16[16,144,512]{2,1,0:T(8,128)(2,1)} %get-tuple-element.62), channel_id=1, source_target_pairs={{0,1},{1,0},{2,3},{3,2},{4,5},{5,4},{6,7},{7,6},{8,9},{9,8},{10,11... | collective-permute-start | bytes 7077896 | tf_op jit(solution)/shard_map/ppermute | solution.py:559
  219.3 66.5 %all-to-all-start.1 = ((bf16[16,144,512]{2,1,0:T(8,128)(2,1)}), bf16[16,144,512]{2,1,0:T(8,128)(2,1)S(1)}, u32[]{:S(2)}, u32[]{:S(2)}) async-start(bf16[16,144,512]{2,1,0:T(8,128)(2,1)} %add_convert_fusion), calls=%async_computation.1 | async-start | bytes 4718592 | tf_op jit(solution)/shard_map/all_to_all | solution.py:661
  224.8 61.8 %copy-start.10 = (f32[1,3584]{1,0:T(1,128)S(1)}, f32[1,3584]{1,0:T(1,128)}, u32[]{:S(2)}) copy-start(f32[1,3584]{1,0:T(1,128)} %get-tuple-element.78) | copy-start | bytes 43012
  285.8 2.6 copy-start.3
  285.8 2.6 collective-permute-start.8
  286.6 1.5 collective-permute-start.9
  287.4 1.5 copy-start.4
  289.1 19.2 %collective-permute-start.12 = (bf16[352,512]{1,0:T(8,128)(2,1)S(1)}, bf16[352,512]{1,0:T(8,128)(2,1)S(1)}, u32[]{:S(2)}, u32[]{:S(2)}) collective-permute-start(bf16[352,512]{1,0:T(8,128)(2,1)S(1)} %get-tuple-element.117), channel_id=1, source_target_pairs={{0,6},{2,4},{4,2},{6,0},{8,14},{10,12},{12,10},{14,8},{16,22},{18,... | collective-permute-start | bytes 1081352 | tf_op jit(solution)/shard_map/ppermute | solution.py:559
  292.0 16.4 %collective-permute-start.11 = (bf16[352,512]{1,0:T(8,128)(2,1)S(1)}, bf16[352,512]{1,0:T(8,128)(2,1)S(1)}, u32[]{:S(2)}, u32[]{:S(2)}) collective-permute-start(bf16[352,512]{1,0:T(8,128)(2,1)S(1)} %get-tuple-element.116), channel_id=1, source_target_pairs={{0,4},{2,6},{4,0},{6,2},{8,12},{10,14},{12,8},{14,10},{16,20},{18,... | collective-permute-start | bytes 1081352 | tf_op jit(solution)/shard_map/ppermute | solution.py:559
  292.5 16.2 %collective-permute-start.10 = (bf16[352,512]{1,0:T(8,128)(2,1)S(1)}, bf16[352,512]{1,0:T(8,128)(2,1)S(1)}, u32[]{:S(2)}, u32[]{:S(2)}) collective-permute-start(bf16[352,512]{1,0:T(8,128)(2,1)S(1)} %get-tuple-element.115), channel_id=1, source_target_pairs={{0,2},{2,0},{4,6},{6,4},{8,10},{10,8},{12,14},{14,12},{16,18},{18,... | collective-permute-start | bytes 1081352 | tf_op jit(solution)/shard_map/ppermute | solution.py:559
  308.9 14.4 %copy-start.12 = (pred[16]{0:T(512)(128)(4,1)S(1)}, pred[16]{0:T(512)(128)(4,1)}, u32[]{:S(2)}) copy-start(pred[16]{0:T(512)(128)(4,1)} %fusion.17) | copy-start | bytes 52
  309.3 7.8 %collective-permute-start.15 = (bf16[112,512]{1,0:T(8,128)(2,1)S(1)}, bf16[112,512]{1,0:T(8,128)(2,1)S(1)}, u32[]{:S(2)}, u32[]{:S(2)}) collective-permute-start(bf16[112,512]{1,0:T(8,128)(2,1)S(1)} %get-tuple-element.114), channel_id=1, source_target_pairs={{0,24},{2,26},{4,28},{6,30},{8,16},{10,18},{12,20},{14,22},{16,8},... | collective-permute-start | bytes 344072 | tf_op jit(solution)/shard_map/ppermute | solution.py:559
  312.6 10.0 %collective-permute-start.14 = (bf16[112,512]{1,0:T(8,128)(2,1)S(1)}, bf16[112,512]{1,0:T(8,128)(2,1)S(1)}, u32[]{:S(2)}, u32[]{:S(2)}) collective-permute-start(bf16[112,512]{1,0:T(8,128)(2,1)S(1)} %get-tuple-element.113), channel_id=1, source_target_pairs={{0,16},{2,18},{4,20},{6,22},{8,24},{10,26},{12,28},{14,30},{16,0},... | collective-permute-start | bytes 344072 | tf_op jit(solution)/shard_map/ppermute | solution.py:559
  312.6 10.0 %collective-permute-start.13 = (bf16[112,512]{1,0:T(8,128)(2,1)S(1)}, bf16[112,512]{1,0:T(8,128)(2,1)S(1)}, u32[]{:S(2)}, u32[]{:S(2)}) collective-permute-start(bf16[112,512]{1,0:T(8,128)(2,1)S(1)} %get-tuple-element.112), channel_id=1, source_target_pairs={{0,8},{2,10},{4,12},{6,14},{8,0},{10,2},{12,4},{14,6},{16,24},{18,... | collective-permute-start | bytes 344072 | tf_op jit(solution)/shard_map/ppermute | solution.py:559
  322.7 7.0 %copy-start.2 = (f32[112,512]{1,0:T(8,128)}, f32[112,512]{1,0:T(8,128)S(1)}, u32[]{:S(2)}) copy-start(f32[112,512]{1,0:T(8,128)S(1)} %convert_add_fusion.1.sums_ref) | copy-start | bytes 688132
  324.1 20.7 %all-to-all-start.2 = ((bf16[16,16,512]{2,1,0:T(8,128)(2,1)}), bf16[16,16,512]{2,1,0:T(8,128)(2,1)S(1)}, u32[]{:S(2)}, u32[]{:S(2)}) async-start(bf16[16,16,512]{2,1,0:T(8,128)(2,1)} %select_select_fusion), calls=%async_computation.2 | async-start | bytes 524288 | tf_op jit(solution)/shard_map/all_to_all | solution.py:692
  329.7 14.6 %copy-start.7 = (f32[4608]{0:T(1024)S(1)}, f32[4608]{0:T(1024)}, u32[]{:S(2)}) copy-start(f32[4608]{0:T(1024)} %param.15) | copy-start | bytes 55300
  329.7 14.6 %copy-start.8 = (f32[4608]{0:T(1024)S(1)}, f32[4608]{0:T(1024)}, u32[]{:S(2)}) copy-start(f32[4608]{0:T(1024)} %param.16) | copy-start | bytes 55300
  329.7 14.6 %copy-start.9 = (f32[4608]{0:T(1024)S(1)}, f32[4608]{0:T(1024)}, u32[]{:S(2)}) copy-start(f32[4608]{0:T(1024)} %param.17) | copy-start | bytes 55300
  329.7 15.2 %copy-start.1 = (f32[1,256,512]{2,1,0:T(8,128)S(1)}, f32[1,256,512]{2,1,0:T(8,128)}, u32[]{:S(2)}) copy-start(f32[1,256,512]{2,1,0:T(8,128)} %param.12) | copy-start | bytes 1572868
  329.7 15.2 %copy-start.5 = (f32[1,256,512]{2,1,0:T(8,128)S(1)}, f32[1,256,512]{2,1,0:T(8,128)}, u32[]{:S(2)}) copy-start(f32[1,256,512]{2,1,0:T(8,128)} %param.14) | copy-start | bytes 1572868
  329.7 15.2 %copy-start.6 = (f32[1,256,512]{2,1,0:T(8,128)S(1)}, f32[1,256,512]{2,1,0:T(8,128)}, u32[]{:S(2)}) copy-start(f32[1,256,512]{2,1,0:T(8,128)} %param.13) | copy-start | bytes 1572868
Sparse Core Ops, SparseCore 0:
  10.9 83.1 all-gather.2

commit v2 on v1

--- a/solution.py
+++ b/solution.py
@@ -646,7 +646,10 @@
     owned = jnp.any(names, 1)
     block_of = jnp.argmax(names, 1)
     place = jnp.stack([me, lax.axis_index("narrow")]).astype(jnp.int32)
-    place, small, owned, block_of, tokens = lax.optimization_barrier((place, small, owned, block_of, tokens))
+    owns_slot = owned[me]
+    place, small, owned, owns_slot, block_of, tokens = lax.optimization_barrier(
+        (place, small, owned, owns_slot, block_of, tokens)
+    )
     normal, scale, means = norm_call(tokens)
     parts, mean_all = fetch_blocks(low_master, owner_list[:3], means, groups is not None)
     queries, keys, values, weights, attended, inverse, sum_k, sum_v = attend_call(
@@ -693,7 +696,6 @@
     grad_tokens = last_call(normal, scale, d_low, d_branch, far, cuts[0], small)
     moved, grad_tokens = tie((moved, grad_tokens))
     own_grad = moved.reshape(1, -1, D).astype(F32)
-    owns_slot = owned[me]
     slot_weight, slot_first, slot_second = adamw_update(
         master, own_grad, moment_one, moment_two, 0.1, RATE
     )

time: 355 us -> 354 us (level)
  no operation moved by 1% of the time
where the time goes in v2:
time: 354 us
  Pallas kernels  243 us (69%)
  waiting for transfers between devices  40.2 us (11%)
  starting transfers between devices  35.8 us (10%)
  between operations  14.5 us (4%)
  other arithmetic  13.8 us (4%)
  local copies, waits for them, and re-layouts  6.42 us (2%)
    pallas_call x1, Pallas kernels, ff_call(): pl.pallas_call(functools.partial(ff_kernel, groups is not None), grid_spe...  107 us
    pallas_call x1, Pallas kernels, back_call(): pl.pallas_call(functools.partial(back_kernel, groups is not None), grid_s...  60.9 us
    ppermute x16, waiting for transfers between devices, swap(): lax.ppermute(value, axis, [(index, index ^ bit) for index in range(size)])  40.1 us
    pallas_call x1, Pallas kernels, attend_call(): pl.pallas_call(functools.partial(attend_kernel, len(parts)), grid_spec=pl...  34.4 us
    ppermute x16, starting transfers between devices, swap(): lax.ppermute(value, axis, [(index, index ^ bit) for index in range(size)])  16.8 us
    pallas_call x1, Pallas kernels, low_call(): pl.pallas_call(low_kernel, grid_spec=pltpu.PrefetchScalarGridSpec(num_sca...  15.6 us
    pallas_call x1, Pallas kernels, last_call(): pl.pallas_call(functools.partial(last_kernel, start, count // ROW), grid=...  14.5 us
    pallas_call x1, Pallas kernels, norm_call(): pl.pallas_call(norm_kernel, grid=(images,), in_specs=[tile_spec(count, D)...  10.1 us
  transfers between devices with their start and end apart: 20, of which 13 were waited for; matrix products, arithmetic and copies ran while one was open for 3% of the time, Pallas kernels for 38%

profile of v2, /device:TPU:0, one launch (start us, length us, event | category | flops | bytes accessed | tf_op | source)
XLA Modules:
  0.0 353.5 jit_solution(16879721854125614482)
XLA Ops:
  7.2 1.8 convert_element_type.82
  9.0 8.3 %all-to-all-start = ((bf16[16,16,512]{2,1,0:T(8,128)(2,1)}), bf16[16,16,512]{2,1,0:T(8,128)(2,1)S(1)}, u32[]{:S(2)}, u32[]{:S(2)}) async-start(bf16[16,16,512]{2,1,0:T(8,128)(2,1)} %bitcast.60), calls=%async_computation | async-start | bytes 524288 | tf_op jit(solution)/shard_map/all_to_all | solution.py:587
  17.4 1.3 iota_reduce_fusion
  18.7 0.8 fusion.17
  19.4 1.3 reshape.141.params_ref.refs_10_
  20.8 0.6 dynamic_slice.3
  21.4 0.7 pad_add_fusion.place
  22.1 10.1 %norm_one.1 = (bf16[8,768,512]{2,1,0:T(8,128)(2,1)}, f32[8,768,1]{2,1,0:T(8,128)}, bf16[8,4,512]{2,1,0:T(4,128)(2,1)}) custom-call(bf16[8,768,512]{2,1,0:T(8,128)(2,1)} %x_ref.1), custom_call_target="tpu_custom_call" | custom-call | flops 31457280 | bytes 12582912 | tf_op jit(solution)/shard_map/norm_one/pallas_call | solution.py:94
  32.2 0.8 reshape.143
  33.2 0.6 gather_fusion
  33.9 3.8 %collective-permute-start.2 = (bf16[80,512]{1,0:T(8,128)(2,1)S(1)}, bf16[80,512]{1,0:T(8,128)(2,1)S(1)}, u32[]{:S(2)}, u32[]{:S(2)}) collective-permute-start(bf16[80,512]{1,0:T(8,128)(2,1)S(1)} %get-tuple-element.113), channel_id=1, source_target_pairs={{0,24},{2,26},{4,28},{6,30},{8,16},{10,18},{12,20},{14,22},{16,8},... | collective-permute-start | bytes 245768 | tf_op jit(solution)/shard_map/ppermute | solution.py:559
  37.7 0.6 collective-permute-start
  38.3 2.8 collective-permute-done.2
  41.2 6.0 %collective-permute-done.1 = bf16[80,512]{1,0:T(8,128)(2,1)S(1)} collective-permute-done((bf16[80,512]{1,0:T(8,128)(2,1)S(1)}, bf16[80,512]{1,0:T(8,128)(2,1)S(1)}, u32[]{:S(2)}, u32[]{:S(2)}) %collective-permute-start.1) | collective-permute-done | bytes 81952 | tf_op jit(solution)/shard_map/ppermute | solution.py:559
  47.2 2.4 collective-permute-start.5
  49.6 0.5 collective-permute-start.4
  50.2 0.6 collective-permute-start.3
  50.8 8.1 %collective-permute-done.5 = bf16[4,80,512]{2,1,0:T(8,128)(2,1)S(1)} collective-permute-done((bf16[4,80,512]{2,1,0:T(8,128)(2,1)S(1)}, bf16[4,80,512]{2,1,0:T(8,128)(2,1)S(1)}, u32[]{:S(2)}, u32[]{:S(2)}) %collective-permute-start.5) | collective-permute-done | bytes 327712 | tf_op jit(solution)/shard_map/ppermute | solution.py:559
  58.9 4.6 %collective-permute-done.4 = bf16[4,80,512]{2,1,0:T(8,128)(2,1)S(1)} collective-permute-done((bf16[4,80,512]{2,1,0:T(8,128)(2,1)S(1)}, bf16[4,80,512]{2,1,0:T(8,128)(2,1)S(1)}, u32[]{:S(2)}, u32[]{:S(2)}) %collective-permute-start.4) | collective-permute-done | bytes 327712 | tf_op jit(solution)/shard_map/ppermute | solution.py:559
  64.1 0.2 copy.27
  64.3 0.9 reshape.146.mean_ref.refs_9_
  65.2 3.5 %collective-permute-done.6.refs_1_ = bf16[16,80,512]{2,1,0:T(8,128)(2,1)} collective-permute-done((bf16[16,80,512]{2,1,0:T(8,128)(2,1)S(1)}, bf16[16,80,512]{2,1,0:T(8,128)(2,1)}, u32[]{:S(2)}, u32[]{:S(2)}) %collective-permute-start.6) | collective-permute-done | bytes 1310752 | tf_op jit(solution)/shard_map/ppermute | solution.py:559
  68.8 34.4 %attend.1 = (bf16[8,768,512]{2,1,0:T(8,128)(2,1)}, bf16[8,768,512]{2,1,0:T(8,128)(2,1)}, bf16[8,768,512]{2,1,0:T(8,128)(2,1)}, bf16[8,4,8,192,256]{4,3,2,1,0:T(8...) custom-call(s32[2]{0:T(128)} %pad_add_fusion.place, ...), custom_call_target="tpu_custom_call" | custom-call | flops 16106127360 | bytes 62914560 | tf_op jit(solution)/shard_map/attend/pallas_call | solution.py:208
  103.2 107.3 %feed_forward.1 = (bf16[8,768,512]{2,1,0:T(8,128)(2,1)}, bf16[8,768,512]{2,1,0:T(8,128)(2,1)}, bf16[8,768,512]{2,1,0:T(8,128)(2,1)}, f32[1,3584]{1,0:T(1,128)}, ...) custom-call(s32[12]{0:T(128)} %owner.5, s32[2]{0:T(128)} %pad_add_fusion.place, bf16[8,768,512]{2,1,0:T(8,128)(2,1)} %x_ref.1, ...), custom_call_target="tpu_custom_call" | custom-call | flops 86973087744 | bytes 44040192 | tf_op jit(solution)/shard_map/feed_forward/pallas_call | solution.py:337
  210.5 0.2 collective-permute-start.7
  210.7 4.6 %collective-permute-done.7 = bf16[16,144,512]{2,1,0:T(8,128)(2,1)S(1)} collective-permute-done((bf16[16,144,512]{2,1,0:T(8,128)(2,1)}, bf16[16,144,512]{2,1,0:T(8,128)(2,1)S(1)}, u32[]{:S(2)}, u32[]{:S(2)}) %collective-permute-start.7) | collective-permute-done | bytes 2359328 | tf_op jit(solution)/shard_map/ppermute | solution.py:559
  215.3 3.8 %add_convert_fusion = bf16[16,144,512]{2,1,0:T(8,128)(2,1)} fusion(bf16[16,144,512]{2,1,0:T(8,128)(2,1)S(1)} %collective-permute-done.7, bf16[16,144,512]{2,1,0:T(8,128)(2,1)} %get-tuple-element.62), kind=kLoop, calls=%fused_computation.3 | loop fusion | flops 4718592 | bytes 7077888 | tf_op jit(solution)/shard_map/convert_element_type | solution.py:620
  219.1 5.7 %all-to-all-start.1 = ((bf16[16,144,512]{2,1,0:T(8,128)(2,1)}), bf16[16,144,512]{2,1,0:T(8,128)(2,1)S(1)}, u32[]{:S(2)}, u32[]{:S(2)}) async-start(bf16[16,144,512]{2,1,0:T(8,128)(2,1)} %add_convert_fusion), calls=%async_computation.1 | async-start | bytes 4718592 | tf_op jit(solution)/shard_map/all_to_all | solution.py:664
  224.8 60.9 %attend_back.1 = (bf16[8,768,1536]{2,1,0:T(8,128)(2,1)}, bf16[4,4,32,512]{3,2,1,0:T(8,128)(2,1)}, f32[1,1024]{1,0:T(1,128)}, bf16[4,4,48,512]{3,2,1,0:T(8,128)(2,1)}, bf16[4,4,48,512]{3,2,1,0:T(8,128)(2,1)}) custom-call(s32[12]{0:T(128)} %owner.5, s32[2]{0:T(128)} %pad_add_fusion.place, bf16[8,768,512]{2,1,0:T(8,128)(2,1)} %get-tuple-element.66.refs_0_, ...), custom_call_target="tpu_custom_call" | custom-call | flops 32212254720 | bytes 75497472 | tf_op jit(solution)/shard_map/attend_back/pallas_call | solution.py:464
  285.8 0.7 constant_dynamic-update-slice_fusion.1
  286.6 0.4 collective-permute-start.9
  287.0 0.3 convert_reduce_fusion
  287.3 0.8 collective-permute-done.9
  288.3 0.2 add_convert_fusion.1
  289.0 2.9 collective-permute-start.12
  291.9 0.6 collective-permute-start.11
  292.6 15.6 %project_back.1.low_ref = bf16[8,768,512]{2,1,0:T(8,128)(2,1)} custom-call(s32[12]{0:T(128)} %owner.5, bf16[8,768,1536]{2,1,0:T(8,128)(2,1)} %get-tuple-element.85.grad_ref, bf16[16,512,512]{2,1,0:T(8,128)(2,1)} %bitcast.54, bf16[16,512,512]{2,1,0:T(8,128)(2,1)} %bitcast.55, bf16[16,512,512]{2,1,0:T(8,128)(2,1)} %bitcast.56), custom_call_target="tpu_custom_call" | custom-call | flops 9663676416 | bytes 25165824 | tf_op jit(solution)/shard_map/project_back/pallas_call | solution.py:503
  308.4 0.3 collective-permute-done.10
  309.2 3.3 collective-permute-start.15
  312.6 1.1 collective-permute-start.13
  313.7 3.3 collective-permute-done.15
  317.0 5.6 %collective-permute-done.14 = bf16[112,512]{1,0:T(8,128)(2,1)S(1)} collective-permute-done((bf16[112,512]{1,0:T(8,128)(2,1)S(1)}, bf16[112,512]{1,0:T(8,128)(2,1)S(1)}, u32[]{:S(2)}, u32[]{:S(2)}) %collective-permute-start.14) | collective-permute-done | bytes 114720 | tf_op jit(solution)/shard_map/ppermute | solution.py:559
  322.7 0.6 gather_fusion.1
  323.3 0.8 select_select_fusion
  324.1 4.9 %all-to-all-start.2 = ((bf16[16,16,512]{2,1,0:T(8,128)(2,1)}), bf16[16,16,512]{2,1,0:T(8,128)(2,1)S(1)}, u32[]{:S(2)}, u32[]{:S(2)}) async-start(bf16[16,16,512]{2,1,0:T(8,128)(2,1)} %select_select_fusion), calls=%async_computation.2 | async-start | bytes 524288 | tf_op jit(solution)/shard_map/all_to_all | solution.py:695
  329.1 14.5 %norm_one_back.1 = f32[8,768,512]{2,1,0:T(8,128)} custom-call(bf16[8,768,512]{2,1,0:T(8,128)(2,1)} %get-tuple-element.54.xh_ref.refs_6_, f32[8,768,1]{2,1,0:T(8,128)} %get-tuple-element.88.scale_ref, bf16[8,768,512]{2,1,0:T(8,128)(2,1)} %project_back.1.low_ref, bf16[8,768,512]{2,1,0:T(8,128)(2,1)} %get-tuple-element.90.dr_ref, f32[112,512]{1,0:T(8,128)} %copy-done.2, ...), custom_call_target="tpu_custom_call" | custom-call | flops 62914560 | bytes 34603008 | tf_op jit(solution)/shard_map/norm_one_back/pallas_call | solution.py:535
  343.6 0.6 multiply_subtract_fusion
  344.3 2.4 fusion.3
  (81 shorter events, 2.6 us)
Async XLA Ops:
  7.2 96.0 %all-gather.3.cloned.1.call-start = ((), (), s32[]{:S(2)}) async-start(), calls=%async_computation.3 | async-start | bytes 8650752 | tf_op jit(solution)/shard_map/all_gather | solution.py:638
  9.0 24.2 %all-to-all-start = ((bf16[16,16,512]{2,1,0:T(8,128)(2,1)}), bf16[16,16,512]{2,1,0:T(8,128)(2,1)S(1)}, u32[]{:S(2)}, u32[]{:S(2)}) async-start(bf16[16,16,512]{2,1,0:T(8,128)(2,1)} %bitcast.60), calls=%async_computation | async-start | bytes 524288 | tf_op jit(solution)/shard_map/all_to_all | solution.py:587
  19.4 12.8 %copy-start.12 = (pred[16]{0:T(512)(128)(4,1)}, pred[16]{0:T(512)(128)(4,1)S(1)}, u32[]{:S(2)}) copy-start(pred[16]{0:T(512)(128)(4,1)S(1)} %fusion.17) | copy-start | bytes 52
  22.1 10.9 %copy-start.11 = (s32[12]{0:T(128)S(1)}, s32[12]{0:T(128)}, u32[]{:S(2)}) copy-start(s32[12]{0:T(128)} %owner.5) | copy-start | bytes 148
  33.9 7.3 %collective-permute-start.2 = (bf16[80,512]{1,0:T(8,128)(2,1)S(1)}, bf16[80,512]{1,0:T(8,128)(2,1)S(1)}, u32[]{:S(2)}, u32[]{:S(2)}) collective-permute-start(bf16[80,512]{1,0:T(8,128)(2,1)S(1)} %get-tuple-element.113), channel_id=1, source_target_pairs={{0,24},{2,26},{4,28},{6,30},{8,16},{10,18},{12,20},{14,22},{16,8},... | collective-permute-start | bytes 245768 | tf_op jit(solution)/shard_map/ppermute | solution.py:559
  37.7 9.5 %collective-permute-start.1 = (bf16[80,512]{1,0:T(8,128)(2,1)S(1)}, bf16[80,512]{1,0:T(8,128)(2,1)S(1)}, u32[]{:S(2)}, u32[]{:S(2)}) collective-permute-start(bf16[80,512]{1,0:T(8,128)(2,1)S(1)} %get-tuple-element.113), channel_id=1, source_target_pairs={{0,16},{2,18},{4,20},{6,22},{8,24},{10,26},{12,28},{14,30},{16,0},... | collective-permute-start | bytes 245768 | tf_op jit(solution)/shard_map/ppermute | solution.py:559
  37.7 9.5 %collective-permute-start = (bf16[80,512]{1,0:T(8,128)(2,1)S(1)}, bf16[80,512]{1,0:T(8,128)(2,1)S(1)}, u32[]{:S(2)}, u32[]{:S(2)}) collective-permute-start(bf16[80,512]{1,0:T(8,128)(2,1)S(1)} %get-tuple-element.113), channel_id=1, source_target_pairs={{0,8},{2,10},{4,12},{6,14},{8,0},{10,2},{12,4},{14,6},{16,24},{18,... | collective-permute-start | bytes 245768 | tf_op jit(solution)/shard_map/ppermute | solution.py:559
  47.2 11.7 %collective-permute-start.5 = (bf16[4,80,512]{2,1,0:T(8,128)(2,1)S(1)}, bf16[4,80,512]{2,1,0:T(8,128)(2,1)S(1)}, u32[]{:S(2)}, u32[]{:S(2)}) collective-permute-start(bf16[4,80,512]{2,1,0:T(8,128)(2,1)S(1)} %get-tuple-element.111), channel_id=1, source_target_pairs={{0,6},{2,4},{4,2},{6,0},{8,14},{10,12},{12,10},{14,8},{16,22},{18,... | collective-permute-start | bytes 983048 | tf_op jit(solution)/shard_map/ppermute | solution.py:559
  49.6 13.9 %collective-permute-start.4 = (bf16[4,80,512]{2,1,0:T(8,128)(2,1)S(1)}, bf16[4,80,512]{2,1,0:T(8,128)(2,1)S(1)}, u32[]{:S(2)}, u32[]{:S(2)}) collective-permute-start(bf16[4,80,512]{2,1,0:T(8,128)(2,1)S(1)} %get-tuple-element.111), channel_id=1, source_target_pairs={{0,4},{2,6},{4,0},{6,2},{8,12},{10,14},{12,8},{14,10},{16,20},{18,... | collective-permute-start | bytes 983048 | tf_op jit(solution)/shard_map/ppermute | solution.py:559
  50.2 13.5 %collective-permute-start.3 = (bf16[4,80,512]{2,1,0:T(8,128)(2,1)S(1)}, bf16[4,80,512]{2,1,0:T(8,128)(2,1)S(1)}, u32[]{:S(2)}, u32[]{:S(2)}) collective-permute-start(bf16[4,80,512]{2,1,0:T(8,128)(2,1)S(1)} %get-tuple-element.111), channel_id=1, source_target_pairs={{0,2},{2,0},{4,6},{6,4},{8,10},{10,8},{12,14},{14,12},{16,18},{18,... | collective-permute-start | bytes 983048 | tf_op jit(solution)/shard_map/ppermute | solution.py:559
  63.8 4.9 %copy-start = (bf16[4,4,80,512]{3,2,1,0:T(8,128)(2,1)}, bf16[4,4,80,512]{3,2,1,0:T(8,128)(2,1)S(1)}, u32[]{:S(2)}) copy-start(bf16[4,4,80,512]{3,2,1,0:T(8,128)(2,1)S(1)} %pad_maximum_fusion) | copy-start | bytes 3932164
  63.8 4.9 %collective-permute-start.6 = (bf16[16,80,512]{2,1,0:T(8,128)(2,1)S(1)}, bf16[16,80,512]{2,1,0:T(8,128)(2,1)}, u32[]{:S(2)}, u32[]{:S(2)}) collective-permute-start(bf16[16,80,512]{2,1,0:T(8,128)(2,1)S(1)} %bitcast.57), channel_id=1, source_target_pairs={{0,1},{1,0},{2,3},{3,2},{4,5},{5,4},{6,7},{7,6},{8,9},{9,8},{10,11... | collective-permute-start | bytes 3932168 | tf_op jit(solution)/shard_map/ppermute | solution.py:559
  210.5 4.8 %collective-permute-start.7 = (bf16[16,144,512]{2,1,0:T(8,128)(2,1)}, bf16[16,144,512]{2,1,0:T(8,128)(2,1)S(1)}, u32[]{:S(2)}, u32[]{:S(2)}) collective-permute-start(bf16[16,144,512]{2,1,0:T(8,128)(2,1)} %get-tuple-element.63), channel_id=1, source_target_pairs={{0,1},{1,0},{2,3},{3,2},{4,5},{5,4},{6,7},{7,6},{8,9},{9,8},{10,11... | collective-permute-start | bytes 7077896 | tf_op jit(solution)/shard_map/ppermute | solution.py:559
  219.1 66.7 %all-to-all-start.1 = ((bf16[16,144,512]{2,1,0:T(8,128)(2,1)}), bf16[16,144,512]{2,1,0:T(8,128)(2,1)S(1)}, u32[]{:S(2)}, u32[]{:S(2)}) async-start(bf16[16,144,512]{2,1,0:T(8,128)(2,1)} %add_convert_fusion), calls=%async_computation.1 | async-start | bytes 4718592 | tf_op jit(solution)/shard_map/all_to_all | solution.py:664
  224.8 61.8 %copy-start.10 = (f32[1,3584]{1,0:T(1,128)S(1)}, f32[1,3584]{1,0:T(1,128)}, u32[]{:S(2)}) copy-start(f32[1,3584]{1,0:T(1,128)} %get-tuple-element.79) | copy-start | bytes 43012
  285.7 2.6 copy-start.3
  285.7 2.6 collective-permute-start.8
  286.6 1.5 collective-permute-start.9
  287.3 1.5 copy-start.4
  289.0 19.2 %collective-permute-start.12 = (bf16[352,512]{1,0:T(8,128)(2,1)S(1)}, bf16[352,512]{1,0:T(8,128)(2,1)S(1)}, u32[]{:S(2)}, u32[]{:S(2)}) collective-permute-start(bf16[352,512]{1,0:T(8,128)(2,1)S(1)} %get-tuple-element.119), channel_id=1, source_target_pairs={{0,6},{2,4},{4,2},{6,0},{8,14},{10,12},{12,10},{14,8},{16,22},{18,... | collective-permute-start | bytes 1081352 | tf_op jit(solution)/shard_map/ppermute | solution.py:559
  291.9 16.4 %collective-permute-start.11 = (bf16[352,512]{1,0:T(8,128)(2,1)S(1)}, bf16[352,512]{1,0:T(8,128)(2,1)S(1)}, u32[]{:S(2)}, u32[]{:S(2)}) collective-permute-start(bf16[352,512]{1,0:T(8,128)(2,1)S(1)} %get-tuple-element.118), channel_id=1, source_target_pairs={{0,4},{2,6},{4,0},{6,2},{8,12},{10,14},{12,8},{14,10},{16,20},{18,... | collective-permute-start | bytes 1081352 | tf_op jit(solution)/shard_map/ppermute | solution.py:559
  292.5 16.2 %collective-permute-start.10 = (bf16[352,512]{1,0:T(8,128)(2,1)S(1)}, bf16[352,512]{1,0:T(8,128)(2,1)S(1)}, u32[]{:S(2)}, u32[]{:S(2)}) collective-permute-start(bf16[352,512]{1,0:T(8,128)(2,1)S(1)} %get-tuple-element.117), channel_id=1, source_target_pairs={{0,2},{2,0},{4,6},{6,4},{8,10},{10,8},{12,14},{14,12},{16,18},{18,... | collective-permute-start | bytes 1081352 | tf_op jit(solution)/shard_map/ppermute | solution.py:559
  308.9 14.4 %copy-start.13 = (pred[16]{0:T(512)(128)(4,1)S(1)}, pred[16]{0:T(512)(128)(4,1)}, u32[]{:S(2)}) copy-start(pred[16]{0:T(512)(128)(4,1)} %copy-done.12) | copy-start | bytes 52
  309.2 7.8 %collective-permute-start.15 = (bf16[112,512]{1,0:T(8,128)(2,1)S(1)}, bf16[112,512]{1,0:T(8,128)(2,1)S(1)}, u32[]{:S(2)}, u32[]{:S(2)}) collective-permute-start(bf16[112,512]{1,0:T(8,128)(2,1)S(1)} %get-tuple-element.116), channel_id=1, source_target_pairs={{0,24},{2,26},{4,28},{6,30},{8,16},{10,18},{12,20},{14,22},{16,8},... | collective-permute-start | bytes 344072 | tf_op jit(solution)/shard_map/ppermute | solution.py:559
  312.6 10.0 %collective-permute-start.14 = (bf16[112,512]{1,0:T(8,128)(2,1)S(1)}, bf16[112,512]{1,0:T(8,128)(2,1)S(1)}, u32[]{:S(2)}, u32[]{:S(2)}) collective-permute-start(bf16[112,512]{1,0:T(8,128)(2,1)S(1)} %get-tuple-element.115), channel_id=1, source_target_pairs={{0,16},{2,18},{4,20},{6,22},{8,24},{10,26},{12,28},{14,30},{16,0},... | collective-permute-start | bytes 344072 | tf_op jit(solution)/shard_map/ppermute | solution.py:559
  312.6 10.0 %collective-permute-start.13 = (bf16[112,512]{1,0:T(8,128)(2,1)S(1)}, bf16[112,512]{1,0:T(8,128)(2,1)S(1)}, u32[]{:S(2)}, u32[]{:S(2)}) collective-permute-start(bf16[112,512]{1,0:T(8,128)(2,1)S(1)} %get-tuple-element.114), channel_id=1, source_target_pairs={{0,8},{2,10},{4,12},{6,14},{8,0},{10,2},{12,4},{14,6},{16,24},{18,... | collective-permute-start | bytes 344072 | tf_op jit(solution)/shard_map/ppermute | solution.py:559
  322.7 6.4 %copy-start.2 = (f32[112,512]{1,0:T(8,128)}, f32[112,512]{1,0:T(8,128)S(1)}, u32[]{:S(2)}) copy-start(f32[112,512]{1,0:T(8,128)S(1)} %convert_add_fusion.1.sums_ref) | copy-start | bytes 688132
  324.1 20.1 %all-to-all-start.2 = ((bf16[16,16,512]{2,1,0:T(8,128)(2,1)}), bf16[16,16,512]{2,1,0:T(8,128)(2,1)S(1)}, u32[]{:S(2)}, u32[]{:S(2)}) async-start(bf16[16,16,512]{2,1,0:T(8,128)(2,1)} %select_select_fusion), calls=%async_computation.2 | async-start | bytes 524288 | tf_op jit(solution)/shard_map/all_to_all | solution.py:695
  329.0 14.6 %copy-start.7 = (f32[4608]{0:T(1024)S(1)}, f32[4608]{0:T(1024)}, u32[]{:S(2)}) copy-start(f32[4608]{0:T(1024)} %param.15) | copy-start | bytes 55300
  329.0 14.6 %copy-start.8 = (f32[4608]{0:T(1024)S(1)}, f32[4608]{0:T(1024)}, u32[]{:S(2)}) copy-start(f32[4608]{0:T(1024)} %param.16) | copy-start | bytes 55300
  329.0 14.6 %copy-start.9 = (f32[4608]{0:T(1024)S(1)}, f32[4608]{0:T(1024)}, u32[]{:S(2)}) copy-start(f32[4608]{0:T(1024)} %param.17) | copy-start | bytes 55300
  329.1 15.2 %copy-start.1 = (f32[1,256,512]{2,1,0:T(8,128)S(1)}, f32[1,256,512]{2,1,0:T(8,128)}, u32[]{:S(2)}) copy-start(f32[1,256,512]{2,1,0:T(8,128)} %param.12) | copy-start | bytes 1572868
  329.1 15.2 %copy-start.5 = (f32[1,256,512]{2,1,0:T(8,128)S(1)}, f32[1,256,512]{2,1,0:T(8,128)}, u32[]{:S(2)}) copy-start(f32[1,256,512]{2,1,0:T(8,128)} %param.14) | copy-start | bytes 1572868
  329.1 15.2 %copy-start.6 = (f32[1,256,512]{2,1,0:T(8,128)S(1)}, f32[1,256,512]{2,1,0:T(8,128)}, u32[]{:S(2)}) copy-start(f32[1,256,512]{2,1,0:T(8,128)} %param.13) | copy-start | bytes 1572868
Sparse Core Ops, SparseCore 0:
  10.9 82.9 all-gather.2
